TPU v7x, 32 devices: a whole 2x2x4 slice. The times are simulated.
32 devices in a mesh: ha: 4 (over y, x), wa: 4 (over z), ta: 2 (over core).
Axes of the slice: x: 2, y: 2, z: 4, core: 2. Of those that a mesh axis runs over, the one named last changes fastest.
Arguments:
- hidden_states: bfloat16 [2, 96, 32, 5120], P(None, 'ha', 'wa', 'ta'), may hold values from -60 to 60
- queries: bfloat16 [2, 96, 32, 5120], P(None, 'ha', 'wa', 'ta'), may hold values from -120 to 120
- keys_values: bfloat16 [2, 2, 96, 32, 5120], P(None, None, 'ha', 'wa', 'ta'), may hold values from -16 to 16
- out_weight: bfloat16 [5120, 5120], P('ta', 'wa'), may hold values from -0.078125 to 0.078125
- mod_table: float32 [50, 3, 5120], P(None, None, 'ta'), may hold values from -4 to 4
- windows: int32 [40, 2], P('ta'), may hold values from 0 to 1, as said below
- step_index: int32 [1], replicated, may hold values from 0 to 49
Outputs:
- residual_out: bfloat16 [2, 96, 32, 5120], P(None, 'ha', 'wa', 'ta')
- ffn_input: bfloat16 [2, 96, 32, 5120], P(None, 'ha', 'wa', 'ta')
Inputs may be any that keep to these rules, and one draw needn't show every extreme that they name: `windows`: some head has both radii equal to 1.
All inputs are finite; a program needn't handle non-finite values.
Results may differ from a plain program's by a relative error of at most 0.0085.
Values may be sent and summed in bfloat16 or wider, within the bound.
No kernel may reach another device: no remote copies, remote signals or barrier semaphores. Data moves between devices by JAX's collectives and lax.ppermute only.
A program may use at most 128 MiB of HBM per device.

v0:
```python
from functools import partial
from functools import reduce
import math

import jax
import jax.numpy as jnp
from jax import lax
from jax.sharding import PartitionSpec as P

D = 5120
HD = 128
TILE = 8


EPSILON = 1e-06


def padded_2(block, sides, width):
    for axis, dim in sides:
        count = lax.axis_size(axis)
        forward = [(i, i + 1) for i in range(count - 1)]
        backward = [(target, source) for source, target in forward]
        low = lax.ppermute(
            lax.slice_in_dim(block, block.shape[dim] - width, None, axis=dim), axis, forward
        )
        high = lax.ppermute(lax.slice_in_dim(block, 0, width, axis=dim), axis, backward)
        block = jnp.concatenate([low, block, high], axis=dim)
    return block


def key_set(block, first_row, first_col, placing):
    row_base, col_base, rows_total, cols_total, query_trow, query_tcol = placing
    grid_shape = (block.shape[1], block.shape[2], block.shape[3])
    global_row = row_base + (first_row - TILE) + lax.broadcasted_iota(jnp.int32, grid_shape, 1)
    global_col = col_base + (first_col - TILE) + lax.broadcasted_iota(jnp.int32, grid_shape, 2)
    inside = (
        (global_row >= 0)
        & (global_row < rows_total)
        & (global_col >= 0)
        & (global_col < cols_total)
    ).reshape(-1)
    row_gap = jnp.abs(jnp.floor_divide(global_row, TILE).reshape(-1)[None, :] - query_trow[:, None])
    col_gap = jnp.abs(jnp.floor_divide(global_col, TILE).reshape(-1)[None, :] - query_tcol[:, None])
    entries = grid_shape[0] * grid_shape[1] * grid_shape[2]
    feature_count = block.shape[4]
    return (
        block[0].reshape(entries, feature_count),
        block[1].reshape(entries, feature_count),
        row_gap,
        col_gap,
        inside,
    )


def head_output(index, key_sets, query_rows, windows, head_size):
    radius_row = windows[index, 0]
    radius_col = windows[index, 1]
    query_head = lax.dynamic_slice_in_dim(query_rows, index * head_size, head_size, 1)
    scale = 1.0 / math.sqrt(HD)
    masked = []
    value_heads = []
    for keys_all, values_all, row_gap, col_gap, inside in key_sets:
        key_head = lax.dynamic_slice_in_dim(keys_all, index * head_size, head_size, 1)
        value_heads.append(lax.dynamic_slice_in_dim(values_all, index * head_size, head_size, 1))
        raw = (
            lax.dot_general(
                query_head, key_head, (((1,), (1,)), ((), ())), preferred_element_type=jnp.float32
            )
            * scale
        )
        allowed = inside[None, :] & (row_gap <= radius_row) & (col_gap <= radius_col)
        masked.append(jnp.where(allowed, raw, -jnp.inf))
    highest = reduce(jnp.maximum, [jnp.max(scores, axis=1) for scores in masked])
    expos = [jnp.exp(scores - highest[:, None]) for scores in masked]
    total = reduce(jnp.add, [jnp.sum(expo, axis=1) for expo in expos])
    output = reduce(
        jnp.add,
        [
            jnp.dot(
                (expo / total[:, None]).astype(jnp.bfloat16),
                value_head,
                preferred_element_type=jnp.float32,
            )
            for expo, value_head in zip(expos, value_heads)
        ],
    )
    return output.astype(jnp.bfloat16)


def group_sum(terms):
    return lax.psum_scatter(
        terms.astype(jnp.bfloat16), "ta", scatter_dimension=1, tiled=True
    ).astype(jnp.float32)


def shards(hidden_states, queries, keys_values, out_weight, mod_table, windows, step_index):
    frame_count, row_count, col_count, feature_count = queries.shape
    head_count = windows.shape[0]
    head_size = feature_count // head_count
    token_count = frame_count * row_count * col_count
    row_base = lax.axis_index("ha") * row_count
    col_base = lax.axis_index("wa") * col_count
    rows_total = row_count * lax.axis_size("ha")
    cols_total = col_count * lax.axis_size("wa")
    grid_shape = (frame_count, row_count, col_count)
    query_trow = jnp.floor_divide(
        row_base + lax.broadcasted_iota(jnp.int32, grid_shape, 1), TILE
    ).reshape(-1)
    query_tcol = jnp.floor_divide(
        col_base + lax.broadcasted_iota(jnp.int32, grid_shape, 2), TILE
    ).reshape(-1)
    placing = (row_base, col_base, rows_total, cols_total, query_trow, query_tcol)
    query_rows = queries.reshape(token_count, feature_count)
    padded = padded_2(keys_values, (("ha", 2), ("wa", 3)), TILE)
    key_sets = [key_set(padded, 0, 0, placing)]
    heads_out = lax.map(
        partial(
            head_output,
            key_sets=key_sets,
            query_rows=query_rows,
            windows=windows,
            head_size=head_size,
        ),
        jnp.arange(head_count, dtype=jnp.int32),
    )
    piece = lax.all_gather(out_weight, "wa", axis=1, tiled=True)
    terms = jnp.einsum(
        "htd,hdc->tc",
        heads_out,
        piece.reshape(head_count, head_size, piece.shape[1]),
        preferred_element_type=jnp.float32,
    )
    summed = group_sum(terms)
    select = lax.broadcasted_iota(jnp.int32, (mod_table.shape[0], 1, 1), 0) == step_index[0]
    picked = jnp.sum(jnp.where(select, mod_table, 0.0), axis=0)
    local_width = hidden_states.shape[3]
    mixed = hidden_states.reshape(token_count, local_width).astype(jnp.float32) + picked[0] * summed
    sum_first, sum_second = lax.psum((jnp.sum(mixed, axis=1), jnp.sum(mixed * mixed, axis=1)), "ta")
    average = (sum_first / D)[:, None]
    variance = (sum_second / D)[:, None] - average * average
    normed = (mixed - average) * lax.rsqrt(variance + EPSILON)
    ffn_input = (normed * (1.0 + picked[2]) + picked[1]).astype(jnp.bfloat16)
    residual_out = mixed.astype(jnp.bfloat16)
    out_shape = (frame_count, row_count, col_count, local_width)
    return (residual_out.reshape(out_shape), ffn_input.reshape(out_shape))


def solution(mesh):
    return jax.shard_map(
        shards,
        mesh=mesh,
        in_specs=(
            P(None, "ha", "wa", "ta"),
            P(None, "ha", "wa", "ta"),
            P(None, None, "ha", "wa", "ta"),
            P("ta", "wa"),
            P(None, None, "ta"),
            P("ta", None),
            P(),
        ),
        out_specs=(P(None, "ha", "wa", "ta"), P(None, "ha", "wa", "ta")),
        check_vma=False,
    )
```

profile of v0, /device:TPU:17, one launch (start us, length us, event | category | flops | bytes accessed | tf_op | source)
XLA Modules:
  0.0 775.5 jit_solution(4424615754952904178)
XLA Ops:
  14.5 26.0 %collective-permute-done = bf16[2,2,8,8,2560]{4,3,2,1,0:T(8,128)(2,1)S(1)} collective-permute-done((bf16[2,2,8,8,2560]{4,3,2,1,0:T(8,128)(2,1)S(1)}, bf16[2,2,8,8,2560]{4,3,2,1,0:T(8,128)(2,1)S(1)}, u32[]{:S(2)}, u32[]{:S(2)}) %collective-permute-start) | collective-permute-done | bytes 1310752 | tf_op jit(solution)/shard_map/ppermute | solution.py:23
  43.9 26.8 %collective-permute-done.1 = bf16[2,2,8,8,2560]{4,3,2,1,0:T(8,128)(2,1)S(1)} collective-permute-done((bf16[2,2,8,8,2560]{4,3,2,1,0:T(8,128)(2,1)S(1)}, bf16[2,2,8,8,2560]{4,3,2,1,0:T(8,128)(2,1)S(1)}, u32[]{:S(2)}, u32[]{:S(2)}) %collective-permute-start.1) | collective-permute-done | bytes 1310752 | tf_op jit(solution)/shard_map/ppermute | solution.py:26
  77.9 419.0 %collective-permute-done.2 = bf16[2,2,40,8,2560]{4,3,2,1,0:T(8,128)(2,1)} collective-permute-done((bf16[2,2,40,8,2560]{4,3,2,1,0:T(8,128)(2,1)}, bf16[2,2,40,8,2560]{4,3,2,1,0:T(8,128)(2,1)}, u32[]{:S(2)}, u32[]{:S(2)}) %collective-permute-start.2) | collective-permute-done | bytes 6553632 | tf_op jit(solution)/shard_map/ppermute | solution.py:23
  496.9 9.3 %pad_maximum_fusion = bf16[2,2,40,24,2560]{4,3,2,1,0:T(8,128)(2,1)S(1)} fusion(bf16[2,2,40,8,2560]{4,3,2,1,0:T(8,128)(2,1)} %collective-permute-done.3, bf16[2,2,40,8,2560]{4,3,2,1,0:T(8,128)(2,1)} %constant_dynamic-update-slice_fusion, bf16[2,2,40,8,2560]{4,3,2,1,0:T(8,128)(2,1)} %collective-permute-done.2), kind=kLoop, calls=%fused_computation.24 | loop fusion | flops 58982400 | bytes 39321600 | tf_op jit(solution)/shard_map/concatenate | solution.py:27
  506.2 6.9 fusion.25
  513.1 212.3 %while.11 = (s32[]{:T(128)}, bf16[20,384,128]{2,1,0:T(8,128)(2,1)S(1)}, s32[20]{0:T(128)S(1)}, s32[20,2]{0,1:T(2,128)S(1)}, bf16[384,2560]{1,0:T(8,128)(2,1)}, /...) while((s32[]{:T(128)}, ...), condition=%wide.region_4.5_spmd.clone, body=%wide.region_1.4_spmd.clone.sunk | while | flops 389336064 | bytes 10064761 | solution.py:116
  538.4 4.3 fusion.34
  549.0 4.3 fusion.34
  559.6 4.3 fusion.34
  570.2 4.3 fusion.34
  580.8 4.3 fusion.34
  591.4 4.3 fusion.34
  602.1 4.3 fusion.34
  623.3 4.3 fusion.34
  633.9 4.3 fusion.34
  644.5 4.3 fusion.34
  655.1 4.3 fusion.34
  665.7 4.3 fusion.34
  687.0 4.3 fusion.34
  697.6 4.3 fusion.34
  708.2 4.3 fusion.34
  725.4 15.3 %bitcast_convert_fusion = bf16[384,5120]{1,0:T(8,128)(2,1)} fusion(bf16[20,384,128]{2,1,0:T(8,128)(2,1)S(1)} %get-tuple-element.54, bf16[20,128,5120]{2,1,0:T(8,128)(2,1)} %bitcast.37), kind=kOutput, calls=%fused_computation.25 | convolution fusion | flops 10068295680 | bytes 32112640 | tf_op jit(solution)/shard_map/htd,hdc->tc/dot_general | solution.py:127
  743.4 15.5 %reduce-scatter.2.cloned.1.call-done = bf16[384,2560]{1,0:T(8,128)(2,1)} async-done(((bf16[384,5120]{1,0:T(8,128)(2,1)}), bf16[384,2560]{1,0:T(8,128)(2,1)}) %reduce-scatter.2.cloned.1.call-update) | async-done | bytes 1966096 | tf_op jit(solution)/shard_map/reduce_scatter | solution.py:91
  763.9 4.8 add_convert_fusion
  (170 shorter events, 120.0 us)
Async XLA Ops:
  7.2 718.3 %all-gather.2.cloned.1.call-start = ((), (), s32[]{:S(2)}) async-start(), calls=%async_computation.1 | async-start | bytes 32768000 | tf_op jit(solution)/shard_map/all_gather | solution.py:126
  7.9 751.0 %reduce-scatter.2.cloned.1.call-start = ((), (), s32[]{:S(2)}) async-start(), calls=%async_computation.2 | async-start | bytes 5898240 | tf_op jit(solution)/shard_map/reduce_scatter | solution.py:91
  7.9 33.8 %copy-start = (bf16[2,2,24,8,2560]{4,3,2,1,0:T(8,128)(2,1)S(1)}, bf16[2,2,24,8,2560]{4,3,2,1,0:T(8,128)(2,1)}, u32[]{:S(2)}) copy-start(bf16[2,2,24,8,2560]{4,3,2,1,0:T(8,128)(2,1)} %param.11) | copy-start | bytes 11796484
  10.0 30.6 %collective-permute-start = (bf16[2,2,8,8,2560]{4,3,2,1,0:T(8,128)(2,1)S(1)}, bf16[2,2,8,8,2560]{4,3,2,1,0:T(8,128)(2,1)S(1)}, u32[]{:S(2)}, u32[]{:S(2)}) collective-permute-start(bf16[2,2,8,8,2560]{4,3,2,1,0:T(8,128)(2,1)S(1)} %get-tuple-element.138), channel_id=1, source_target_pairs={{0,8},{8,16},{16,24},{1,9},{9,17},{17,25},{2,10},{10,18},{18,26},{... | collective-permute-start | bytes 3932168 | tf_op jit(solution)/shard_map/ppermute | solution.py:23
  13.2 57.5 %collective-permute-start.1 = (bf16[2,2,8,8,2560]{4,3,2,1,0:T(8,128)(2,1)S(1)}, bf16[2,2,8,8,2560]{4,3,2,1,0:T(8,128)(2,1)S(1)}, u32[]{:S(2)}, u32[]{:S(2)}) collective-permute-start(bf16[2,2,8,8,2560]{4,3,2,1,0:T(8,128)(2,1)S(1)} %get-tuple-element.137), channel_id=1, source_target_pairs={{8,0},{16,8},{24,16},{9,1},{17,9},{25,17},{10,2},{18,10},{26,18},{... | collective-permute-start | bytes 3932168 | tf_op jit(solution)/shard_map/ppermute | solution.py:26
  71.9 425.1 %collective-permute-start.2 = (bf16[2,2,40,8,2560]{4,3,2,1,0:T(8,128)(2,1)}, bf16[2,2,40,8,2560]{4,3,2,1,0:T(8,128)(2,1)}, u32[]{:S(2)}, u32[]{:S(2)}) collective-permute-start(bf16[2,2,40,8,2560]{4,3,2,1,0:T(8,128)(2,1)} %constant_dynamic-update-slice_fusion), channel_id=1, source_target_pairs={{0,2},{2,4},{4,6},{1,3},{3,5},{5,7},{8,10},{10,12},{12,14},{9,11},... | collective-permute-start | bytes 19660808 | tf_op jit(solution)/shard_map/ppermute | solution.py:23
  75.1 421.9 %collective-permute-start.3 = (bf16[2,2,40,8,2560]{4,3,2,1,0:T(8,128)(2,1)}, bf16[2,2,40,8,2560]{4,3,2,1,0:T(8,128)(2,1)}, u32[]{:S(2)}, u32[]{:S(2)}) collective-permute-start(bf16[2,2,40,8,2560]{4,3,2,1,0:T(8,128)(2,1)} %constant_dynamic-update-slice_fusion), channel_id=1, source_target_pairs={{2,0},{4,2},{6,4},{3,1},{5,3},{7,5},{10,8},{12,10},{14,12},{11,9},... | collective-permute-start | bytes 19660808 | tf_op jit(solution)/shard_map/ppermute | solution.py:26
  506.2 6.9 copy-start.2
  740.8 18.1 %copy-start.1 = (bf16[2,24,8,2560]{3,2,1,0:T(8,128)(2,1)S(1)}, bf16[2,24,8,2560]{3,2,1,0:T(8,128)(2,1)}, u32[]{:S(2)}) copy-start(bf16[2,24,8,2560]{3,2,1,0:T(8,128)(2,1)} %param.9) | copy-start | bytes 5898244
Sparse Core Ops, SparseCore 0:
  9.6 581.7 all-gather.1
  740.9 17.9 reduce-scatter.1
where the time goes:
time: 779 us; the launch traced here: 776 us
  waiting for transfers between devices  488 us (63%)
  matrix products  136 us (17%)
  loops' own time  52.4 us (7%)
  local copies, waits for them, and re-layouts  40.4 us (5%)
  other arithmetic  31.2 us (4%)
  between operations  15 us (2%)
  starting transfers between devices  9.84 us (1%)
    ppermute x2, waiting for transfers between devices, padded_2(): lax.ppermute(lax.slice_in_dim(block, block.shape[dim] - width, None, axis...  445 us
    dot_general x20, matrix products, head_output(): lax.dot_general(query_head, key_head, (((1,), (1,)), ((), ())), preferred...  86 us
    another operation x1, loops' own time, shards(): lax.map(partial(head_output, key_sets=key_sets, query_rows=query_rows, wi...  52.4 us
    dot_general x20, matrix products, head_output(): jnp.dot((expo / total[:, None]).astype(jnp.bfloat16), value_head, preferr...  34.7 us
    ppermute x2, waiting for transfers between devices, padded_2(): lax.ppermute(lax.slice_in_dim(block, 0, width, axis=dim), axis, backward)  26.8 us
  transfers between devices with their start and end apart: 6, of which 4 were waited for; matrix products, arithmetic and copies ran while one was open for 24% of the time, Pallas kernels for 0%

commit v1 on v0

v1 whole, which is shorter than its diff:
```python
from functools import partial
import math

import jax
import jax.numpy as jnp
from jax import lax
from jax.experimental import pallas as pl
from jax.experimental.pallas import tpu as pltpu
from jax.sharding import PartitionSpec as P

D = 5120
HD = 128
TILE = 8

EPSILON = 1e-06
VMEM_LIMIT = 56 * 1024 * 1024


def kernel_params():
    return pltpu.CompilerParams(
        dimension_semantics=("arbitrary",), vmem_limit_bytes=VMEM_LIMIT
    )


def attention_kernel(windows, edges, *refs, q_count, columns_only):
    q_refs = refs[:q_count]
    kv_ref, top_ref, bottom_ref = refs[q_count : q_count + 3]
    out_refs = refs[q_count + 3 : 2 * q_count + 3]
    stat_refs = refs[2 * q_count + 3 :]
    frames, tokens, head_size = q_refs[0].shape
    span = top_ref.shape[2]
    tiles = tokens // span
    head = pl.program_id(0)
    radius_row = windows[head, 0]
    radius_col = windows[head, 1]
    scale = 1.0 / math.sqrt(HD)

    @pl.when(head == 0)
    def _():
        for stat_ref in stat_refs:
            stat_ref[...] = jnp.zeros_like(stat_ref)

    def near(which, tile, wide):
        if not wide:
            return kv_ref[which, :, tile * span : (tile + 1) * span, :].reshape(-1, head_size)
        pieces = []
        if tile == 0:
            pieces.append(top_ref[which])
        low = max(tile - 1, 0) * span
        high = min(tile + 2, tiles) * span
        pieces.append(kv_ref[which, :, low:high, :])
        if tile == tiles - 1:
            pieces.append(bottom_ref[which])
        block = pieces[0] if len(pieces) == 1 else jnp.concatenate(pieces, axis=1)
        return block.reshape(-1, head_size)

    def attend(wide):
        lane = lax.broadcasted_iota(jnp.int32, (frames, span, stat_refs[0].shape[2]), 2)
        for tile in range(tiles):
            rows = slice(tile * span, (tile + 1) * span)
            keys = near(0, tile, wide)
            values = near(1, tile, wide)
            bias = None
            if wide and (tile == 0 or tile == tiles - 1):
                place = lax.rem(
                    lax.broadcasted_iota(jnp.int32, (1, keys.shape[0]), 1), 3 * span
                )
                low = jnp.where(edges[0] == 0, span, 0) if tile == 0 else 0
                high = jnp.where(edges[1] == 0, 2 * span, 3 * span) if tile == tiles - 1 else 3 * span
                bias = jnp.where((place >= low) & (place < high), 0.0, -jnp.inf)
            for q_ref, out_ref, stat_ref in zip(q_refs, out_refs, stat_refs):
                query = q_ref[:, rows, :].reshape(-1, head_size)
                scores = (
                    lax.dot_general(
                        query, keys, (((1,), (1,)), ((), ())), preferred_element_type=jnp.float32
                    )
                    * scale
                )
                if bias is not None:
                    scores = scores + bias
                highest = jnp.max(scores, axis=1, keepdims=True)
                expo = jnp.exp(scores - highest)
                total = jnp.sum(expo, axis=1, keepdims=True)
                output = jnp.dot(
                    expo.astype(jnp.bfloat16), values, preferred_element_type=jnp.float32
                ) * (1.0 / total)
                out_ref[:, rows, :] = output.astype(jnp.bfloat16).reshape(frames, span, head_size)
                level = (highest + jnp.log(total)).reshape(frames, span, 1)
                stat_ref[:, rows, :] = jnp.where(lane == head, level, stat_ref[:, rows, :])

    if columns_only:

        @pl.when(radius_col == 0)
        def _():
            for out_ref in out_refs:
                out_ref[...] = jnp.zeros_like(out_ref)

        active = radius_col != 0
    else:
        active = True

    @pl.when(jnp.logical_and(active, radius_row == 0))
    def _():
        attend(False)

    @pl.when(jnp.logical_and(active, radius_row != 0))
    def _():
        attend(True)


def attention(windows, edges, query_blocks, keys_values, top, bottom, columns_only):
    frames, tokens, features = query_blocks[0].shape
    head_count = windows.shape[0]
    head_size = features // head_count
    span = top.shape[2]
    q_count = len(query_blocks)
    lanes = 128
    q_spec = pl.BlockSpec((frames, tokens, head_size), lambda h, *_: (0, 0, h))
    kv_spec = pl.BlockSpec((2, frames, tokens, head_size), lambda h, *_: (0, 0, 0, h))
    halo_spec = pl.BlockSpec((2, frames, span, head_size), lambda h, *_: (0, 0, 0, h))
    stat_spec = pl.BlockSpec((frames, tokens, lanes), lambda h, *_: (0, 0, 0))
    flops = 4 * q_count * frames * tokens * 2 * frames * span * head_size * head_count
    outs = pl.pallas_call(
        partial(attention_kernel, q_count=q_count, columns_only=columns_only),
        grid_spec=pltpu.PrefetchScalarGridSpec(
            num_scalar_prefetch=2,
            grid=(head_count,),
            in_specs=[q_spec] * q_count + [kv_spec, halo_spec, halo_spec],
            out_specs=[q_spec] * q_count + [stat_spec] * q_count,
        ),
        out_shape=[jax.ShapeDtypeStruct((frames, tokens, features), jnp.bfloat16)] * q_count
        + [jax.ShapeDtypeStruct((frames, tokens, lanes), jnp.float32)] * q_count,
        compiler_params=kernel_params(),
        cost_estimate=pl.CostEstimate(
            flops=flops, bytes_accessed=12_000_000, transcendentals=flops // 256
        ),
        name="attend_neighbours" if columns_only else "attend_own",
    )(windows, edges, *query_blocks, keys_values, top, bottom)
    return outs[:q_count], outs[q_count:]


def combine_kernel(windows, edges, own, left, right, own_stat, left_stat, right_stat, out):
    head = pl.program_id(0)
    radius_col = windows[head, 1]

    @pl.when(radius_col == 0)
    def _():
        out[...] = own[...]

    @pl.when(radius_col != 0)
    def _():
        lane = lax.broadcasted_iota(jnp.int32, own_stat.shape, 2)

        def level(ref):
            return jnp.sum(jnp.where(lane == head, ref[...], 0.0), axis=2, keepdims=True)

        own_level = level(own_stat)
        left_level = jnp.where(edges[2] == 0, -jnp.inf, level(left_stat))
        right_level = jnp.where(edges[3] == 0, -jnp.inf, level(right_stat))
        highest = jnp.maximum(own_level, jnp.maximum(left_level, right_level))
        weights = [jnp.exp(x - highest) for x in (own_level, left_level, right_level)]
        inverse = 1.0 / (weights[0] + weights[1] + weights[2])
        mixed = sum(
            ref[...].astype(jnp.float32) * (weight * inverse)
            for ref, weight in zip((own, left, right), weights)
        )
        out[...] = mixed.astype(jnp.bfloat16)


def combine(windows, edges, outputs, stats):
    frames, tokens, features = outputs[0].shape
    head_count = windows.shape[0]
    head_size = features // head_count
    spec = pl.BlockSpec((frames, tokens, head_size), lambda h, *_: (0, 0, h))
    stat_spec = pl.BlockSpec(stats[0].shape, lambda h, *_: (0, 0, 0))
    return pl.pallas_call(
        combine_kernel,
        grid_spec=pltpu.PrefetchScalarGridSpec(
            num_scalar_prefetch=2,
            grid=(head_count,),
            in_specs=[spec] * 3 + [stat_spec] * 3,
            out_specs=spec,
        ),
        out_shape=jax.ShapeDtypeStruct((frames, tokens, features), jnp.bfloat16),
        compiler_params=kernel_params(),
        cost_estimate=pl.CostEstimate(
            flops=10 * frames * tokens * features,
            bytes_accessed=8 * frames * tokens * features,
            transcendentals=0,
        ),
        name="combine",
    )(windows, edges, *outputs, *stats)


def project_kernel(first, attended, weight, out):
    depth = weight.shape[2]
    total = None
    for part in range(weight.shape[0]):
        term = jnp.dot(
            attended[:, part * depth : (part + 1) * depth],
            weight[part, 0],
            preferred_element_type=jnp.float32,
        )
        total = term if total is None else total + term
    out[0] = total.astype(jnp.bfloat16)


def project(attended, weights, first, count):
    parts, _, depth, width = weights.shape
    tokens, features = attended.shape
    return pl.pallas_call(
        project_kernel,
        grid_spec=pltpu.PrefetchScalarGridSpec(
            num_scalar_prefetch=1,
            grid=(count,),
            in_specs=[
                pl.BlockSpec((tokens, features), lambda i, first: (0, 0)),
                pl.BlockSpec((parts, 1, depth, width), lambda i, first: (0, first[0] + i, 0, 0)),
            ],
            out_specs=pl.BlockSpec((1, tokens, width), lambda i, first: (i, 0, 0)),
        ),
        out_shape=jax.ShapeDtypeStruct((count, tokens, width), jnp.bfloat16),
        compiler_params=kernel_params(),
        cost_estimate=pl.CostEstimate(
            flops=2 * tokens * features * width * count,
            bytes_accessed=2 * features * width * count,
            transcendentals=0,
        ),
        name="project",
    )(first, attended, weights)


def shift(block, axis, step):
    count = lax.axis_size(axis)
    pairs = [(i, i + step) for i in range(count) if 0 <= i + step < count]
    return lax.ppermute(block, axis, pairs)


def shards(hidden_states, queries, keys_values, out_weight, mod_table, windows, step_index):
    frames, rows, cols, features = queries.shape
    n_ha, n_wa, n_ta = lax.axis_size("ha"), lax.axis_size("wa"), lax.axis_size("ta")
    ha, wa, ta = lax.axis_index("ha"), lax.axis_index("wa"), lax.axis_index("ta")
    tokens = frames * rows * cols

    depth = features // n_ha
    share = lax.dynamic_slice_in_dim(out_weight, ha * depth, depth, 0)
    weights = lax.all_gather(share, ("ha", "wa"), axis=0, tiled=False).reshape(
        n_ha, n_wa, depth, out_weight.shape[1]
    )

    edges = jnp.stack([ha > 0, ha < n_ha - 1, wa > 0, wa < n_wa - 1]).astype(jnp.int32)
    top = shift(keys_values[:, :, rows - TILE :], "ha", 1)
    bottom = shift(keys_values[:, :, :TILE], "ha", -1)
    from_left = shift(queries, "wa", 1)
    from_right = shift(queries, "wa", -1)

    def flat(block):
        return block.reshape(block.shape[:-3] + (-1, features))

    kv, top, bottom = flat(keys_values), flat(top), flat(bottom)
    (own,), (own_stat,) = attention(windows, edges, [flat(queries)], kv, top, bottom, False)
    (for_left, for_right), (left_stat, right_stat) = attention(
        windows, edges, [flat(from_left), flat(from_right)], kv, top, bottom, True
    )
    left, left_level = shift(for_right, "wa", 1), shift(right_stat, "wa", 1)
    right, right_level = shift(for_left, "wa", -1), shift(left_stat, "wa", -1)
    attended = combine(
        windows, edges, [own, left, right], [own_stat, left_level, right_level]
    ).reshape(tokens, features)

    blocks = n_wa // n_ta
    summed = None
    for step in list(range(1, n_ta)) + [0]:
        target = lax.rem(ta + step, n_ta)
        piece = project(attended, weights, (target * blocks).reshape(1), blocks)
        if step:
            piece = lax.ppermute(piece, "ta", [(i, (i + step) % n_ta) for i in range(n_ta)])
        piece = piece.astype(jnp.float32)
        summed = piece if summed is None else summed + piece
    width = hidden_states.shape[3]
    summed = jnp.transpose(summed, (1, 0, 2)).reshape(tokens, width)

    picked = lax.dynamic_index_in_dim(mod_table, step_index[0], 0, keepdims=False)
    mixed = hidden_states.reshape(tokens, width).astype(jnp.float32) + picked[0] * summed
    sum_first, sum_second = lax.psum((jnp.sum(mixed, axis=1), jnp.sum(mixed * mixed, axis=1)), "ta")
    average = (sum_first / D)[:, None]
    variance = (sum_second / D)[:, None] - average * average
    normed = (mixed - average) * lax.rsqrt(variance + EPSILON)
    ffn_input = (normed * (1.0 + picked[2]) + picked[1]).astype(jnp.bfloat16)
    residual_out = mixed.astype(jnp.bfloat16)
    out_shape = (frames, rows, cols, width)
    return (residual_out.reshape(out_shape), ffn_input.reshape(out_shape))


def solution(mesh):
    return jax.shard_map(
        shards,
        mesh=mesh,
        in_specs=(
            P(None, "ha", "wa", "ta"),
            P(None, "ha", "wa", "ta"),
            P(None, None, "ha", "wa", "ta"),
            P("ta", "wa"),
            P(None, None, "ta"),
            P("ta", None),
            P(),
        ),
        out_specs=(P(None, "ha", "wa", "ta"), P(None, "ha", "wa", "ta")),
        check_vma=False,
    )
```

time: 779 us -> 425 us (0.55)
  waiting for transfers between devices: 488 us -> 263 us
  matrix products: 136 us -> 0 us
  Pallas kernels: 0 us -> 88.7 us
  loops' own time: 52.4 us -> 0 us
  local copies, waits for them, and re-layouts: 40.4 us -> 19.7 us
  other arithmetic: 31.2 us -> 11.8 us
  starting transfers between devices: 9.84 us -> 22.4 us
    ppermute x4 -> x9, waiting for transfers between devices: 472 us -> 131 us  [the longest x8 131 us: shift(): return lax.ppermute(block, axis, pairs)]
    dot_general x41 -> x0, matrix products: 136 us -> none  [the longest x20 86 us: head_output(): lax.dot_general(query_head, key_head, (((1,), (1,)), ((), ())), preferred...]
    all_gather x1, waiting for transfers between devices: 0.02 us -> 133 us  [shards(): lax.all_gather(share, ('ha', 'wa'), axis=0, tiled=False)]
    pallas_call x0 -> x5, Pallas kernels: none -> 88.7 us  [the longest x2 50.8 us: attention(): pl.pallas_call(partial(attention_kernel, q_count=q_count, columns_only=co...]
    another operation x1 -> x0, loops' own time: 52.4 us -> none  [shards(): lax.map(partial(head_output, key_sets=key_sets, query_rows=query_rows, wi...]
    dynamic_slice x40 -> x1, local copies, waits for them, and re-layouts: 24.6 us -> 2.85 us  [shards(): share = lax.dynamic_slice_in_dim(out_weight, ha * depth, depth, 0)]
    reduce_scatter x1 -> x0, waiting for transfers between devices: 15.5 us -> none  [group_sum(): lax.psum_scatter(terms.astype(jnp.bfloat16), 'ta', scatter_dimension=1, t...]
    reduce_sum x21 -> x0, other arithmetic: 12.8 us -> none  [the longest x20 11 us: head_output(): total = reduce(jnp.add, [jnp.sum(expo, axis=1) for expo in expos])]
  transfers between devices with their start and end apart: 6 -> 10, of which waited for: 4 -> 6; matrix products, arithmetic and copies ran while one was open for 24% -> 1% of each run, Pallas kernels for 0% -> 18%
where the time goes in v1:
time: 425 us; the launch traced here: 423 us
  waiting for transfers between devices  263 us (62%)
  Pallas kernels  88.7 us (21%)
  starting transfers between devices  22.4 us (5%)
  local copies, waits for them, and re-layouts  19.7 us (5%)
  between operations  14.9 us (4%)
  other arithmetic  11.8 us (3%)
    all_gather x1, waiting for transfers between devices, shards(): lax.all_gather(share, ('ha', 'wa'), axis=0, tiled=False)  133 us
    ppermute x8, waiting for transfers between devices, shift(): return lax.ppermute(block, axis, pairs)  131 us
    pallas_call x2, Pallas kernels, attention(): pl.pallas_call(partial(attention_kernel, q_count=q_count, columns_only=co...  50.8 us
    pallas_call x2, Pallas kernels, project(): pl.pallas_call(project_kernel, grid_spec=pltpu.PrefetchScalarGridSpec(num...  21.7 us
    ppermute x8, starting transfers between devices, shift(): return lax.ppermute(block, axis, pairs)  21.3 us
    pallas_call x1, Pallas kernels, combine(): pl.pallas_call(combine_kernel, grid_spec=pltpu.PrefetchScalarGridSpec(num...  16.2 us
  transfers between devices with their start and end apart: 10, of which 6 were waited for; matrix products, arithmetic and copies ran while one was open for 1% of the time, Pallas kernels for 18%

profile of v1, /device:TPU:17, one launch (start us, length us, event | category | flops | bytes accessed | tf_op | source)
XLA Modules:
  0.0 423.3 jit_solution(10784799592987470929)
XLA Ops:
  7.2 2.8 constant_dynamic-slice_fusion
  10.1 3.2 collective-permute-start.2
  13.3 2.1 collective-permute-start.3
  15.4 3.4 fusion.3
  18.8 3.2 collective-permute-start
  24.6 37.3 %collective-permute-done = bf16[2,2,8,8,2560]{4,3,2,1,0:T(8,128)(2,1)S(1)} collective-permute-done((bf16[2,2,8,8,2560]{4,3,2,1,0:T(8,128)(2,1)}, bf16[2,2,8,8,2560]{4,3,2,1,0:T(8,128)(2,1)S(1)}, u32[]{:S(2)}, u32[]{:S(2)}) %collective-permute-start) | collective-permute-done | bytes 1310752 | tf_op jit(solution)/shard_map/ppermute | solution.py:236
  61.9 30.0 %collective-permute-done.1 = bf16[2,2,8,8,2560]{4,3,2,1,0:T(8,128)(2,1)} collective-permute-done((bf16[2,2,8,8,2560]{4,3,2,1,0:T(8,128)(2,1)}, bf16[2,2,8,8,2560]{4,3,2,1,0:T(8,128)(2,1)}, u32[]{:S(2)}, u32[]{:S(2)}) %collective-permute-start.1) | collective-permute-done | bytes 1310752 | tf_op jit(solution)/shard_map/ppermute | solution.py:236
  92.1 28.6 %attend_neighbours.1 = (bf16[2,192,2560]{2,1,0:T(8,128)(2,1)}, bf16[2,192,2560]{2,1,0:T(8,128)(2,1)}, f32[2,192,128]{2,1,0:T(8,128)}, f32[2,192,128]{2,1,0:T(8,128)}) custom-call(s32[20,2]{1,0:T(8,128)} %copy.14.windows, s32[4]{0:T(128)} %add_convert_fusion.1.edges, bf16[2,192,2560]{2,1,0:T(8,128)(2,1)} %bitcast.10.refs_0_, ...), custom_call_target="tpu_custom_call" | custom-call | flops 2013265920 | bytes 12000000 | tf_op jit(solution)/shard_map/attend_neighbours/pallas_call | solution.py:123
  120.8 2.9 collective-permute-start.4
  123.6 3.0 collective-permute-start.5
  126.7 3.5 collective-permute-start.6
  130.2 2.1 collective-permute-start.7
  132.3 22.2 %attend_own.1 = (bf16[2,192,2560]{2,1,0:T(8,128)(2,1)}, f32[2,192,128]{2,1,0:T(8,128)}) custom-call(s32[20,2]{1,0:T(8,128)} %copy.14.windows, s32[4]{0:T(128)} %add_convert_fusion.1.edges, bf16[2,192,2560]{2,1,0:T(8,128)(2,1)} %bitcast.26, bf16[2,2,192,2560]{3,2,1,0:T(8,128)(2,1)} %bitcast.25, bf16[2,2,64,2560]{3,2,1,0:T(8,128)(2,1)} %bitcast.28, ...), custom_call_target="tpu_custom_call" | custom-call | flops 1006632960 | bytes 12000000 | tf_op jit(solution)/shard_map/attend_own/pallas_call | solution.py:123
  154.6 62.5 %collective-permute-done.6.left_stat = f32[2,192,128]{2,1,0:T(8,128)S(1)} collective-permute-done((f32[2,192,128]{2,1,0:T(8,128)}, f32[2,192,128]{2,1,0:T(8,128)S(1)}, u32[]{:S(2)}, u32[]{:S(2)}) %collective-permute-start.6) | collective-permute-done | bytes 196640 | tf_op jit(solution)/shard_map/ppermute | solution.py:236
  219.2 16.2 %combine.1 = bf16[2,192,2560]{2,1,0:T(8,128)(2,1)} custom-call(s32[20,2]{1,0:T(8,128)} %copy.14.windows, s32[4]{0:T(128)} %add_convert_fusion.1.edges, bf16[2,192,2560]{2,1,0:T(8,128)(2,1)} %get-tuple-element.8.own, bf16[2,192,2560]{2,1,0:T(8,128)(2,1)} %copy-done.2, bf16[2,192,2560]{2,1,0:T(8,128)(2,1)} %collective-permute-done.5.right, ...), custom_call_target="tpu_custom_call" | custom-call | flops 9830400 | bytes 7864320 | tf_op jit(solution)/shard_map/combine/pallas_call | solution.py:176
  235.4 132.5 %all-gather.3.cloned.1.call-done = bf16[10240,1280]{1,0:T(8,128)(2,1)} async-done(((bf16[640,1280]{1,0:T(8,128)(2,1)}), bf16[10240,1280]{1,0:T(8,128)(2,1)}) %all-gather.3.cloned.1.call-update) | async-done | bytes 26214416 | tf_op jit(solution)/shard_map/all_gather | solution.py:247
  367.9 10.8 %project.2 = bf16[2,384,1280]{2,1,0:T(8,128)(2,1)} custom-call(s32[1]{0:T(128)} %bitcast.1.first, bf16[384,2560]{1,0:T(8,128)(2,1)} %bitcast.22, bf16[4,4,640,1280]{3,2,1,0:T(8,128)(2,1)} %bitcast.20), custom_call_target="tpu_custom_call" | custom-call | flops 5033164800 | bytes 13107200 | tf_op jit(solution)/shard_map/project/pallas_call | solution.py:211
  381.5 10.8 %project.3 = bf16[2,384,1280]{2,1,0:T(8,128)(2,1)} custom-call(s32[1]{0:T(128)} %bitcast.14.first, bf16[384,2560]{1,0:T(8,128)(2,1)} %bitcast.23, bf16[4,4,640,1280]{3,2,1,0:T(8,128)(2,1)} %bitcast.21), custom_call_target="tpu_custom_call" | custom-call | flops 5033164800 | bytes 13107200 | tf_op jit(solution)/shard_map/project/pallas_call | solution.py:211
  392.4 1.9 add_bitcast_fusion
  394.3 4.9 %copy.15 = f32[384,2,1280]{2,1,0:T(2,128)} copy(f32[384,2,1280]{2,0,1:T(8,128)S(1)} %add_bitcast_fusion) | data formatting | bytes 7864320 | tf_op jit(solution)/shard_map/transpose | solution.py:281
  399.2 6.2 %reshape.115 = f32[2,24,8,2560]{3,2,1,0:T(8,128)} reshape(f32[384,2,1280]{2,1,0:T(2,128)} %copy.15) | data formatting | bytes 7864320 | tf_op jit(solution)/shard_map/reshape | solution.py:281
  405.4 3.0 fusion.1
  408.6 2.5 all-reduce
  411.3 5.2 %add_convert_fusion = (bf16[2,24,8,2560]{3,2,1,0:T(8,128)(2,1)}, bf16[2,24,8,2560]{3,2,1,0:T(8,128)(2,1)}) fusion(f32[2560]{0:T(1024)S(1)} %get-tuple-element.18, f32[2560]{0:T(1024)S(1)} %get-tuple-element.16, f32[2,24,8]{2,1,0:T(8,128)S(1)} %mul.59, f32[2,24,8]{2,1,0:T(8,128)S(1)} %sub.15, f32[2,24,8,2560]{3,2,1,0:T(8,128)} %reshape.115, ...), kind=kLoop, calls=%fused_computation | loop fusion | flops 8847360 | bytes 9864192 | tf_op jit(solution)/shard_map/convert_element_type | solution.py:289
  (32 shorter events, 7.5 us)
Async XLA Ops:
  7.2 360.8 %all-gather.3.cloned.1.call-start = ((), (), s32[]{:S(2)}) async-start(), calls=%async_computation | async-start | bytes 27852800 | tf_op jit(solution)/shard_map/all_gather | solution.py:247
  7.2 2.9 copy-start.1
  10.1 13.2 %copy-start.6 = (s32[20,2]{0,1:T(2,128)S(1)}, s32[20,2]{0,1:T(2,128)}, u32[]{:S(2)}) copy-start(s32[20,2]{0,1:T(2,128)} %param.12) | copy-start | bytes 484
  10.1 81.8 %collective-permute-start.2 = (bf16[2,24,8,2560]{3,2,1,0:T(8,128)(2,1)S(1)}, bf16[2,24,8,2560]{3,2,1,0:T(8,128)(2,1)}, u32[]{:S(2)}, u32[]{:S(2)}) collective-permute-start(bf16[2,24,8,2560]{3,2,1,0:T(8,128)(2,1)S(1)} %copy-done.1), channel_id=1, source_target_pairs={{0,2},{2,4},{4,6},{1,3},{3,5},{5,7},{8,10},{10,12},{12,14},{9,11},... | collective-permute-start | bytes 5898248 | tf_op jit(solution)/shard_map/ppermute | solution.py:236
  13.3 78.8 %collective-permute-start.3 = (bf16[2,24,8,2560]{3,2,1,0:T(8,128)(2,1)S(1)}, bf16[2,24,8,2560]{3,2,1,0:T(8,128)(2,1)}, u32[]{:S(2)}, u32[]{:S(2)}) collective-permute-start(bf16[2,24,8,2560]{3,2,1,0:T(8,128)(2,1)S(1)} %copy-done.1), channel_id=1, source_target_pairs={{2,0},{4,2},{6,4},{3,1},{5,3},{7,5},{10,8},{12,10},{14,12},{11,9},... | collective-permute-start | bytes 5898248 | tf_op jit(solution)/shard_map/ppermute | solution.py:236
  18.8 43.1 %collective-permute-start = (bf16[2,2,8,8,2560]{4,3,2,1,0:T(8,128)(2,1)}, bf16[2,2,8,8,2560]{4,3,2,1,0:T(8,128)(2,1)S(1)}, u32[]{:S(2)}, u32[]{:S(2)}) collective-permute-start(bf16[2,2,8,8,2560]{4,3,2,1,0:T(8,128)(2,1)} %get-tuple-element.24), channel_id=1, source_target_pairs={{0,8},{8,16},{16,24},{1,9},{9,17},{17,25},{2,10},{10,18},{18,26},{... | collective-permute-start | bytes 3932168 | tf_op jit(solution)/shard_map/ppermute | solution.py:236
  22.0 69.9 %collective-permute-start.1 = (bf16[2,2,8,8,2560]{4,3,2,1,0:T(8,128)(2,1)}, bf16[2,2,8,8,2560]{4,3,2,1,0:T(8,128)(2,1)}, u32[]{:S(2)}, u32[]{:S(2)}) collective-permute-start(bf16[2,2,8,8,2560]{4,3,2,1,0:T(8,128)(2,1)} %get-tuple-element.23), channel_id=1, source_target_pairs={{8,0},{16,8},{24,16},{9,1},{17,9},{25,17},{10,2},{18,10},{26,18},{... | collective-permute-start | bytes 3932168 | tf_op jit(solution)/shard_map/ppermute | solution.py:236
  61.9 30.2 %copy-start.3 = (bf16[2,2,8,8,2560]{4,3,2,1,0:T(8,128)(2,1)}, bf16[2,2,8,8,2560]{4,3,2,1,0:T(8,128)(2,1)S(1)}, u32[]{:S(2)}) copy-start(bf16[2,2,8,8,2560]{4,3,2,1,0:T(8,128)(2,1)S(1)} %collective-permute-done) | copy-start | bytes 3932164
  120.8 97.1 %collective-permute-start.4 = (bf16[2,192,2560]{2,1,0:T(8,128)(2,1)}, bf16[2,192,2560]{2,1,0:T(8,128)(2,1)S(1)}, u32[]{:S(2)}, u32[]{:S(2)}) collective-permute-start(bf16[2,192,2560]{2,1,0:T(8,128)(2,1)} %get-tuple-element.9), channel_id=1, source_target_pairs={{0,2},{2,4},{4,6},{1,3},{3,5},{5,7},{8,10},{10,12},{12,14},{9,11},... | collective-permute-start | bytes 5898248 | tf_op jit(solution)/shard_map/ppermute | solution.py:236
  123.6 94.2 %collective-permute-start.5 = (bf16[2,192,2560]{2,1,0:T(8,128)(2,1)}, bf16[2,192,2560]{2,1,0:T(8,128)(2,1)}, u32[]{:S(2)}, u32[]{:S(2)}) collective-permute-start(bf16[2,192,2560]{2,1,0:T(8,128)(2,1)} %get-tuple-element.10), channel_id=1, source_target_pairs={{2,0},{4,2},{6,4},{3,1},{5,3},{7,5},{10,8},{12,10},{14,12},{11,9},... | collective-permute-start | bytes 5898248 | tf_op jit(solution)/shard_map/ppermute | solution.py:236
  126.7 90.4 %collective-permute-start.6 = (f32[2,192,128]{2,1,0:T(8,128)}, f32[2,192,128]{2,1,0:T(8,128)S(1)}, u32[]{:S(2)}, u32[]{:S(2)}) collective-permute-start(f32[2,192,128]{2,1,0:T(8,128)} %get-tuple-element.12), channel_id=1, source_target_pairs={{0,2},{2,4},{4,6},{1,3},{3,5},{5,7},{8,10},{10,12},{12,14},{9,11},... | collective-permute-start | bytes 589832 | tf_op jit(solution)/shard_map/ppermute | solution.py:236
  130.2 87.6 %collective-permute-start.7 = (f32[2,192,128]{2,1,0:T(8,128)}, f32[2,192,128]{2,1,0:T(8,128)S(1)}, u32[]{:S(2)}, u32[]{:S(2)}) collective-permute-start(f32[2,192,128]{2,1,0:T(8,128)} %get-tuple-element.13), channel_id=1, source_target_pairs={{2,0},{4,2},{6,4},{3,1},{5,3},{7,5},{10,8},{12,10},{14,12},{11,9},... | collective-permute-start | bytes 589832 | tf_op jit(solution)/shard_map/ppermute | solution.py:236
  217.1 0.8 copy-start.4
  217.8 0.7 copy-start.5
  217.8 1.3 copy-start.2
  378.7 13.6 %collective-permute-start.8 = (bf16[2,384,1280]{2,1,0:T(8,128)(2,1)}, bf16[2,384,1280]{2,1,0:T(8,128)(2,1)S(1)}, u32[]{:S(2)}, u32[]{:S(2)}) collective-permute-start(bf16[2,384,1280]{2,1,0:T(8,128)(2,1)} %project.2), channel_id=1, source_target_pairs={{0,1},{1,0},{2,3},{3,2},{4,5},{5,4},{6,7},{7,6},{8,9},{9,8},{10,11... | collective-permute-start | bytes 5898248 | tf_op jit(solution)/shard_map/ppermute | solution.py:277
  399.2 6.2 %copy-start = (bf16[2,24,8,2560]{3,2,1,0:T(8,128)(2,1)S(1)}, bf16[2,24,8,2560]{3,2,1,0:T(8,128)(2,1)}, u32[]{:S(2)}) copy-start(bf16[2,24,8,2560]{3,2,1,0:T(8,128)(2,1)} %param.7) | copy-start | bytes 5898244
Sparse Core Ops, SparseCore 0:
  10.7 357.1 all-gather.2

commit v2 on v1

v2 whole, which is shorter than its diff:
```python
from functools import partial
import math

import jax
import jax.numpy as jnp
from jax import lax
from jax.experimental import pallas as pl
from jax.experimental.pallas import tpu as pltpu
from jax.sharding import PartitionSpec as P

D = 5120
HD = 128
TILE = 8
LANES = 128
LEVEL_STEP = 32

EPSILON = 1e-06
VMEM_LIMIT = 48 * 1024 * 1024
HEAD_GROUPS = 2


def kernel_params():
    return pltpu.CompilerParams(
        dimension_semantics=("arbitrary",), vmem_limit_bytes=VMEM_LIMIT
    )


def attention_kernel(windows, edges, *refs, q_count, columns_only, first_head, group):
    q_refs = refs[:q_count]
    kv_ref, top_ref, bottom_ref = refs[q_count : q_count + 3]
    out_refs = refs[q_count + 3 : 2 * q_count + 3]
    stat_refs = refs[2 * q_count + 3 :]
    frames, tokens, head_size = q_refs[0].shape
    span = top_ref.shape[2]
    tiles = tokens // span
    step = pl.program_id(0)
    head = first_head + jnp.minimum(step, group - 1)
    radius_row = windows[head, 0]
    radius_col = windows[head, 1]
    scale = 1.0 / math.sqrt(HD)

    @pl.when(step == 0)
    def _():
        for stat_ref in stat_refs:
            stat_ref[...] = jnp.zeros_like(stat_ref)

    def near(which, tile, wide):
        if not wide:
            return kv_ref[which, :, tile * span : (tile + 1) * span, :].reshape(-1, head_size)
        pieces = []
        if tile == 0:
            pieces.append(top_ref[which])
        low = max(tile - 1, 0) * span
        high = min(tile + 2, tiles) * span
        pieces.append(kv_ref[which, :, low:high, :])
        if tile == tiles - 1:
            pieces.append(bottom_ref[which])
        block = pieces[0] if len(pieces) == 1 else jnp.concatenate(pieces, axis=1)
        return block.reshape(-1, head_size)

    def attend(wide):
        lane = lax.broadcasted_iota(jnp.int32, (frames, span, LANES), 2)
        for tile in range(tiles):
            rows = slice(tile * span, (tile + 1) * span)
            keys = near(0, tile, wide)
            values = near(1, tile, wide)
            bias = None
            if wide and (tile == 0 or tile == tiles - 1):
                place = lax.rem(
                    lax.broadcasted_iota(jnp.int32, (1, keys.shape[0]), 1), 3 * span
                )
                low = jnp.where(edges[0] == 0, span, 0) if tile == 0 else 0
                high = jnp.where(edges[1] == 0, 2 * span, 3 * span) if tile == tiles - 1 else 3 * span
                bias = jnp.where((place >= low) & (place < high), 0.0, -jnp.inf)
            for q_ref, out_ref, stat_ref in zip(q_refs, out_refs, stat_refs):
                query = q_ref[:, rows, :].reshape(-1, head_size)
                scores = (
                    lax.dot_general(
                        query, keys, (((1,), (1,)), ((), ())), preferred_element_type=jnp.float32
                    )
                    * scale
                )
                if bias is not None:
                    scores = scores + bias
                highest = jnp.max(scores, axis=1, keepdims=True)
                expo = jnp.exp(scores - highest)
                total = jnp.sum(expo, axis=1, keepdims=True)
                output = jnp.dot(
                    expo.astype(jnp.bfloat16), values, preferred_element_type=jnp.float32
                ) * (1.0 / total)
                out_ref[:, rows, :] = output.astype(jnp.bfloat16).reshape(frames, span, head_size)
                level = (highest + jnp.log(total)).reshape(frames, span, 1)
                stat_ref[:, rows, :] = jnp.where(lane == step, level, stat_ref[:, rows, :])

    active = step < group
    if columns_only:

        @pl.when(active & (radius_col == 0))
        def _():
            for out_ref in out_refs:
                out_ref[...] = jnp.zeros_like(out_ref)

        active = active & (radius_col != 0)

    @pl.when(active & (radius_row == 0))
    def _():
        attend(False)

    @pl.when(active & (radius_row != 0))
    def _():
        attend(True)

    @pl.when(step == group)
    def _():
        for out_ref, stat_ref in zip(out_refs, stat_refs):
            level = stat_ref[...]
            high = level.astype(jnp.bfloat16).astype(jnp.float32)
            middle = (level - high).astype(jnp.bfloat16).astype(jnp.float32)
            low = level - high - middle
            packed = high + pltpu.roll(middle, LEVEL_STEP, 2) + pltpu.roll(low, 2 * LEVEL_STEP, 2)
            out_ref[...] = packed.astype(jnp.bfloat16)


def attention(windows, edges, query_blocks, keys_values, top, bottom, columns_only, first_head, group):
    frames, tokens, features = query_blocks[0].shape
    head_size = features // windows.shape[0]
    span = top.shape[2]
    q_count = len(query_blocks)

    def head_of(step):
        return first_head + jnp.minimum(step, group - 1)

    q_spec = pl.BlockSpec((frames, tokens, head_size), lambda h, *_: (0, 0, head_of(h)))
    kv_spec = pl.BlockSpec((2, frames, tokens, head_size), lambda h, *_: (0, 0, 0, head_of(h)))
    halo_spec = pl.BlockSpec((2, frames, span, head_size), lambda h, *_: (0, 0, 0, head_of(h)))
    out_spec = pl.BlockSpec((frames, tokens, head_size), lambda h, *_: (0, 0, h))
    flops = 4 * q_count * frames * tokens * 2 * frames * span * head_size * group
    return pl.pallas_call(
        partial(
            attention_kernel,
            q_count=q_count,
            columns_only=columns_only,
            first_head=first_head,
            group=group,
        ),
        grid_spec=pltpu.PrefetchScalarGridSpec(
            num_scalar_prefetch=2,
            grid=(group + 1,),
            in_specs=[q_spec] * q_count + [kv_spec, halo_spec, halo_spec],
            out_specs=[out_spec] * q_count,
            scratch_shapes=[pltpu.VMEM((frames, tokens, LANES), jnp.float32)] * q_count,
        ),
        out_shape=[jax.ShapeDtypeStruct((frames, tokens, (group + 1) * head_size), jnp.bfloat16)]
        * q_count,
        compiler_params=kernel_params(),
        cost_estimate=pl.CostEstimate(
            flops=flops, bytes_accessed=20_000_000, transcendentals=flops // 256
        ),
        name="attend_neighbours" if columns_only else "attend_own",
    )(windows, edges, *query_blocks, keys_values, top, bottom)


def combine_kernel(windows, edges, own, left, right, own_stat, left_stat, right_stat, *rest, first_head):
    out = rest[-1]
    step = pl.program_id(0)
    frames, tokens, head_size = own.shape
    radius_col = windows[first_head + step, 1]

    @pl.when(radius_col == 0)
    def _():
        out[...] = own[...]

    @pl.when(radius_col != 0)
    def _():
        lane = lax.broadcasted_iota(jnp.int32, (LANES, head_size), 0)
        pick = jnp.where(
            (lax.rem(lane, LEVEL_STEP) == step) & (lane < 3 * LEVEL_STEP), 1.0, 0.0
        ).astype(jnp.bfloat16)

        def level(ref):
            return jnp.dot(
                ref[...].reshape(-1, LANES), pick, preferred_element_type=jnp.float32
            ).reshape(frames, tokens, head_size)

        own_level = level(own_stat)
        left_level = jnp.where(edges[2] == 0, -jnp.inf, level(left_stat))
        right_level = jnp.where(edges[3] == 0, -jnp.inf, level(right_stat))
        highest = jnp.maximum(own_level, jnp.maximum(left_level, right_level))
        weights = [jnp.exp(x - highest) for x in (own_level, left_level, right_level)]
        mixed = sum(
            ref[...].astype(jnp.float32) * weight for ref, weight in zip((own, left, right), weights)
        )
        out[...] = (mixed / (weights[0] + weights[1] + weights[2])).astype(jnp.bfloat16)


def combine(windows, edges, outputs, first_head, group, features, so_far):
    frames, tokens, _ = outputs[0].shape
    head_size = features // windows.shape[0]
    spec = pl.BlockSpec((frames, tokens, head_size), lambda h, *_: (0, 0, h))
    stat_spec = pl.BlockSpec((frames, tokens, head_size), lambda h, *_: (0, 0, group))
    more = [] if so_far is None else [so_far]
    return pl.pallas_call(
        partial(combine_kernel, first_head=first_head),
        grid_spec=pltpu.PrefetchScalarGridSpec(
            num_scalar_prefetch=2,
            grid=(group,),
            in_specs=[spec] * 3 + [stat_spec] * 3 + [pl.BlockSpec(memory_space=pl.ANY)] * len(more),
            out_specs=pl.BlockSpec((frames, tokens, head_size), lambda h, *_: (0, 0, first_head + h)),
        ),
        out_shape=jax.ShapeDtypeStruct((frames, tokens, features), jnp.bfloat16),
        input_output_aliases={8: 0} if more else {},
        compiler_params=kernel_params(),
        cost_estimate=pl.CostEstimate(
            flops=10 * frames * tokens * head_size * group,
            bytes_accessed=8 * frames * tokens * head_size * group,
            transcendentals=0,
        ),
        name="combine",
    )(windows, edges, *outputs, *outputs, *more)


def project_kernel(starts, attended, *refs, count, carried):
    pieces = refs[:count]
    out = refs[-1]
    total = refs[count][...] if carried else None
    for index, piece in enumerate(pieces):
        start = pl.multiple_of(starts[index], LANES)
        term = jnp.dot(
            attended[:, pl.ds(start, piece.shape[0])],
            piece[...],
            preferred_element_type=jnp.float32,
        )
        total = term if total is None else total + term
    out[...] = total.astype(out.dtype)


def project(attended, pieces, starts, carry, dtype):
    tokens, features = attended.shape
    width = pieces[0].shape[1]
    column = 256 if width % 256 == 0 else width
    depth = sum(piece.shape[0] for piece in pieces)
    out_spec = pl.BlockSpec((tokens, column), lambda i, _: (0, i))
    return pl.pallas_call(
        partial(project_kernel, count=len(pieces), carried=carry is not None),
        grid_spec=pltpu.PrefetchScalarGridSpec(
            num_scalar_prefetch=1,
            grid=(width // column,),
            in_specs=[pl.BlockSpec((tokens, features), lambda i, _: (0, 0))]
            + [pl.BlockSpec((piece.shape[0], column), lambda i, _: (0, i)) for piece in pieces]
            + ([] if carry is None else [out_spec]),
            out_specs=out_spec,
        ),
        out_shape=jax.ShapeDtypeStruct((tokens, width), dtype),
        compiler_params=kernel_params(),
        cost_estimate=pl.CostEstimate(
            flops=2 * tokens * depth * width,
            bytes_accessed=2 * depth * width + 2 * tokens * features,
            transcendentals=0,
        ),
        name="project",
    )(jnp.stack(starts).astype(jnp.int32), attended, *pieces, *([] if carry is None else [carry]))


def mix_kernel(place, own_part, other_part, own_hidden, other_hidden, own_gate, other_gate, *refs):
    mixed_ref, sums_ref = refs[-2:]
    mine = place[0] != 0
    hidden = jnp.where(
        mine, own_hidden[...].astype(jnp.float32), other_hidden[...].astype(jnp.float32)
    )
    gate = jnp.where(mine, own_gate[...], other_gate[...])
    mixed = hidden + gate * (
        own_part[...].astype(jnp.float32) + other_part[...].astype(jnp.float32)
    )
    mixed_ref[...] = mixed
    lane = lax.broadcasted_iota(jnp.int32, sums_ref.shape, 1)
    first = jnp.sum(mixed, axis=1, keepdims=True)
    second = jnp.sum(mixed * mixed, axis=1, keepdims=True)
    sums = jnp.where(lane == 0, first, jnp.where(lane == 1, second, 0.0))
    if len(refs) == 4:
        sums = sums + refs[0][...]
    sums_ref[...] = sums


def mix(place, own_part, other_part, own_hidden, other_hidden, own_gate, other_gate, carry):
    tokens, width = own_part.shape
    blocks = own_hidden.shape[1] // width
    rows = 64 if tokens % 64 == 0 else tokens
    part = pl.BlockSpec((rows, width), lambda i, place: (i, 0))
    hidden = pl.BlockSpec((rows, width), lambda i, place: (i, place[1]))
    gate = pl.BlockSpec((1, width), lambda i, place: (0, place[1]))
    sums = pl.BlockSpec((rows, LANES), lambda i, place: (i, 0))
    mixed = pl.BlockSpec((rows, width), lambda i, place: (i, place[2]))
    more = [] if carry is None else [carry[1], carry[0]]
    return pl.pallas_call(
        mix_kernel,
        grid_spec=pltpu.PrefetchScalarGridSpec(
            num_scalar_prefetch=1,
            grid=(tokens // rows,),
            in_specs=[part, part, hidden, hidden, gate, gate]
            + ([sums, pl.BlockSpec(memory_space=pl.ANY)] if more else []),
            out_specs=[mixed, sums],
        ),
        out_shape=[
            jax.ShapeDtypeStruct((tokens, (blocks + 1) * width), jnp.float32),
            jax.ShapeDtypeStruct((tokens, LANES), jnp.float32),
        ],
        input_output_aliases={8: 0} if more else {},
        compiler_params=kernel_params(),
        cost_estimate=pl.CostEstimate(
            flops=10 * tokens * width, bytes_accessed=12 * tokens * width, transcendentals=0
        ),
        name="mix",
    )(place, own_part, other_part, own_hidden, other_hidden, own_gate, other_gate, *more)


def finish_kernel(
    place, own_part, other_part, own_hidden, other_hidden, own_gate, other_gate, scale, shift_by,
    sums, mixed_ref, residual, ffn,
):
    mine = place[0] != 0
    width = own_part.shape[1]
    blocks = residual.shape[1] // width
    hidden = jnp.where(
        mine, own_hidden[...].astype(jnp.float32), other_hidden[...].astype(jnp.float32)
    )
    gate = jnp.where(mine, own_gate[...], other_gate[...])
    last = hidden + gate * (
        own_part[...].astype(jnp.float32) + other_part[...].astype(jnp.float32)
    )
    first = sums[:, 0:1] + jnp.sum(last, axis=1, keepdims=True)
    second = sums[:, 1:2] + jnp.sum(last * last, axis=1, keepdims=True)
    average = first / D
    variance = second / D - average * average
    inverse = lax.rsqrt(variance + EPSILON)
    for block in range(blocks):
        columns = slice(block * width, (block + 1) * width)
        here = mine & (place[1] == block)
        mixed = jnp.where(here, last, mixed_ref[:, columns])
        residual[:, columns] = mixed.astype(jnp.bfloat16)
        ffn[:, columns] = (
            (mixed - average) * inverse * (1.0 + scale[:, columns]) + shift_by[:, columns]
        ).astype(jnp.bfloat16)


def finish(place, own_part, other_part, own_hidden, other_hidden, own_gate, other_gate, scale, shift_by, carry):
    tokens, width = own_part.shape
    features = own_hidden.shape[1]
    rows = 64 if tokens % 64 == 0 else tokens
    part = pl.BlockSpec((rows, width), lambda i, place: (i, 0))
    hidden = pl.BlockSpec((rows, width), lambda i, place: (i, place[1]))
    gate = pl.BlockSpec((1, width), lambda i, place: (0, place[1]))
    whole = pl.BlockSpec((1, features), lambda i, place: (0, 0))
    sums = pl.BlockSpec((rows, LANES), lambda i, place: (i, 0))
    row = pl.BlockSpec((rows, features), lambda i, place: (i, 0))
    return pl.pallas_call(
        finish_kernel,
        grid_spec=pltpu.PrefetchScalarGridSpec(
            num_scalar_prefetch=1,
            grid=(tokens // rows,),
            in_specs=[part, part, hidden, hidden, gate, gate, whole, whole, sums, row],
            out_specs=[row, row],
        ),
        out_shape=[jax.ShapeDtypeStruct((tokens, features), jnp.bfloat16)] * 2,
        compiler_params=kernel_params(),
        cost_estimate=pl.CostEstimate(
            flops=20 * tokens * features, bytes_accessed=12 * tokens * features, transcendentals=0
        ),
        name="finish",
    )(
        place, own_part, other_part, own_hidden, other_hidden, own_gate, other_gate, scale,
        shift_by, carry[1], carry[0],
    )


def shift(block, axis, step):
    count = lax.axis_size(axis)
    pairs = [(i, i + step) for i in range(count) if 0 <= i + step < count]
    return lax.ppermute(block, axis, pairs)


def turn(block, axis, step):
    count = lax.axis_size(axis)
    return lax.ppermute(block, axis, [(i, (i + step) % count) for i in range(count)])


def swap(block, axis, bit):
    count = lax.axis_size(axis)
    return lax.ppermute(block, axis, [(i, i ^ bit) for i in range(count)])


def attend_all(queries, keys_values, windows):
    frames, rows, cols, features = queries.shape
    n_ha, n_wa = lax.axis_size("ha"), lax.axis_size("wa")
    ha, wa = lax.axis_index("ha"), lax.axis_index("wa")
    head_count = windows.shape[0]

    edges = jnp.stack([ha > 0, ha < n_ha - 1, wa > 0, wa < n_wa - 1]).astype(jnp.int32)
    from_left = shift(queries, "wa", 1)
    from_right = shift(queries, "wa", -1)
    top = shift(keys_values[:, :, rows - TILE :], "ha", 1)
    bottom = shift(keys_values[:, :, :TILE], "ha", -1)

    def flat(block):
        return block.reshape(block.shape[:-3] + (-1, features))

    held = flat(keys_values), flat(top), flat(bottom)
    groups = HEAD_GROUPS if head_count % HEAD_GROUPS == 0 else 1
    group = head_count // groups
    far = []
    for first in range(0, head_count, group):
        for_left, for_right = attention(
            windows, edges, [flat(from_left), flat(from_right)], *held, True, first, group
        )
        far.append((shift(for_right, "wa", 1), shift(for_left, "wa", -1)))
    near = [
        attention(windows, edges, [flat(queries)], *held, False, first, group)[0]
        for first in range(0, head_count, group)
    ]
    attended = None
    for index, first in enumerate(range(0, head_count, group)):
        attended = combine(
            windows, edges, [near[index], *far[index]], first, group, features, attended
        )
    return attended.reshape(-1, features)


def gather_slots(out_weight):
    n_wa = lax.axis_size("wa")
    ha = lax.axis_index("ha")
    depth = out_weight.shape[0] // lax.axis_size("ha")
    half = max(depth * 3 // 5 // LANES, 1) * LANES
    cuts = [(0, half), (half, depth)] if half < depth else [(0, depth)]
    held = [
        lax.dynamic_slice_in_dim(out_weight, ha * depth + low, high - low, 0) for low, high in cuts
    ]
    slots = []
    for _ in range(1, n_wa):
        slot = []
        for index, (low, high) in enumerate(cuts):
            held[index] = turn(held[index], "wa", 1)
            mine = held[index]
            by_x = swap(mine, "ha", 1)
            by_y = swap(mine, "ha", 2)
            split = LANES if high - low > LANES else (high - low) // 2
            far_x = swap(by_y[:split], "ha", 1)
            far_y = swap(by_x[split:], "ha", 2)
            slot.append(
                [
                    (mine, ha * depth + low),
                    (by_x, (ha ^ 1) * depth + low),
                    (by_y, (ha ^ 2) * depth + low),
                    (far_x, (ha ^ 3) * depth + low),
                    (far_y, (ha ^ 3) * depth + low + split),
                ]
            )
        slots.append(slot)
    return slots


def paired(hidden, attended, out_weight, picked):
    n_wa = lax.axis_size("wa")
    wa, ta = lax.axis_index("wa"), lax.axis_index("ta")
    blocks = n_wa // 2
    other_hidden = swap(hidden, "ta", 1)
    gate = picked[0:1]
    other_gate = swap(gate, "ta", 1)
    slots = [[[(out_weight, jnp.int32(0))]]] + gather_slots(out_weight)
    carry = None
    for distance, slot in enumerate(slots):
        block = lax.rem(wa - distance + n_wa, n_wa)
        mine = block // blocks == ta
        inner = lax.rem(block, blocks)
        place = jnp.stack([mine.astype(jnp.int32), inner, jnp.where(mine, inner, blocks)])
        total = None
        for index, part in enumerate(slot):
            dtype = jnp.bfloat16 if index == len(slot) - 1 else jnp.float32
            total = project(attended, [p for p, _ in part], [s for _, s in part], total, dtype)
        other = swap(total, "ta", 1)
        operands = (place, total, other, hidden, other_hidden, gate, other_gate)
        if distance < n_wa - 1:
            carry = mix(*operands, carry)
    return finish(*operands, picked[2:3], picked[1:2], carry)


def gathered(hidden, attended, out_weight, picked):
    n_ha, n_wa, n_ta = lax.axis_size("ha"), lax.axis_size("wa"), lax.axis_size("ta")
    ha, ta = lax.axis_index("ha"), lax.axis_index("ta")
    tokens, features = attended.shape
    depth = features // n_ha
    width = out_weight.shape[1]
    share = lax.dynamic_slice_in_dim(out_weight, ha * depth, depth, 0)
    weights = lax.all_gather(share, ("ha", "wa"), axis=0, tiled=False).reshape(
        n_ha, n_wa, depth, width
    )
    partial_sums = jnp.einsum(
        "thk,hwkc->wtc",
        attended.reshape(tokens, n_ha, depth),
        weights,
        preferred_element_type=jnp.float32,
    ).astype(jnp.bfloat16)
    blocks = n_wa // n_ta
    summed = None
    for step in range(n_ta):
        target = lax.rem(ta + step, n_ta)
        piece = lax.dynamic_slice_in_dim(partial_sums, target * blocks, blocks, 0)
        if step:
            piece = turn(piece, "ta", step)
        piece = piece.astype(jnp.float32)
        summed = piece if summed is None else summed + piece
    summed = jnp.transpose(summed, (1, 0, 2)).reshape(tokens, -1)
    mixed = hidden.astype(jnp.float32) + picked[0] * summed
    sum_first, sum_second = lax.psum((jnp.sum(mixed, axis=1), jnp.sum(mixed * mixed, axis=1)), "ta")
    average = (sum_first / D)[:, None]
    variance = (sum_second / D)[:, None] - average * average
    normed = (mixed - average) * lax.rsqrt(variance + EPSILON)
    ffn_input = (normed * (1.0 + picked[2]) + picked[1]).astype(jnp.bfloat16)
    return mixed.astype(jnp.bfloat16), ffn_input


def shards(hidden_states, queries, keys_values, out_weight, mod_table, windows, step_index):
    tokens = math.prod(queries.shape[:3])
    width = hidden_states.shape[3]
    picked = lax.dynamic_index_in_dim(mod_table, step_index[0], 0, keepdims=False)
    attended = attend_all(queries, keys_values, windows)
    regular = lax.axis_size("ta") == 2 and lax.axis_size("ha") == 4 and width % LANES == 0
    residual_out, ffn_input = (paired if regular else gathered)(
        hidden_states.reshape(tokens, width), attended, out_weight, picked
    )
    return residual_out.reshape(hidden_states.shape), ffn_input.reshape(hidden_states.shape)


def solution(mesh):
    return jax.shard_map(
        shards,
        mesh=mesh,
        in_specs=(
            P(None, "ha", "wa", "ta"),
            P(None, "ha", "wa", "ta"),
            P(None, None, "ha", "wa", "ta"),
            P("ta", "wa"),
            P(None, None, "ta"),
            P("ta", None),
            P(),
        ),
        out_specs=(P(None, "ha", "wa", "ta"), P(None, "ha", "wa", "ta")),
        check_vma=False,
    )
```

time: 425 us -> 393 us (0.925)
  waiting for transfers between devices: 263 us -> 155 us
  starting transfers between devices: 22.4 us -> 66.9 us
  Pallas kernels: 88.7 us -> 129 us
  local copies, waits for them, and re-layouts: 19.7 us -> 35 us
  between operations: 14.9 us -> 1.81 us
  other arithmetic: 11.8 us -> 0.38 us
    all_gather x1 -> x0, waiting for transfers between devices: 133 us -> none  [shards(): lax.all_gather(share, ('ha', 'wa'), axis=0, tiled=False)]
    ppermute x1 -> x36, waiting for transfers between devices: 0.01 us -> 120 us  [the longest x6 77.6 us: turn(): lax.ppermute(block, axis, [(i, (i + step) % count) for i in range(count)])]
    ppermute x8, waiting for transfers between devices: 131 us -> 35.6 us  [shift(): return lax.ppermute(block, axis, pairs)]
    ppermute x1 -> x36, starting transfers between devices: 1.08 us -> 46.3 us  [the longest x30 39.7 us: swap(): return lax.ppermute(block, axis, [(i, i ^ bit) for i in range(count)])]
    pallas_call x3 -> x13, Pallas kernels: 37.9 us -> 79.7 us  [the longest x7 44.3 us: project(): pl.pallas_call(partial(project_kernel, count=len(pieces), carried=carry i...]
    unnamed x15 -> x75, local copies, waits for them, and re-layouts: 2.04 us -> 16.1 us
    slice x1 -> x14, local copies, waits for them, and re-layouts: 3.37 us -> 16.2 us  [the longest x6 7.31 us: gather_slots(): far_y = swap(by_x[split:], 'ha', 2)]
    reshape x1 -> x0, local copies, waits for them, and re-layouts: 6.21 us -> none  [shards(): summed = jnp.transpose(summed, (1, 0, 2)).reshape(tokens, width)]
  transfers between devices with their start and end apart: 10 -> 44, of which waited for: 6 -> 10; matrix products, arithmetic and copies ran while one was open for 1% -> 4% of each run, Pallas kernels for 18% -> 31%
where the time goes in v2:
time: 393 us; the launch traced here: 388 us
  waiting for transfers between devices  155 us (39%)
  Pallas kernels  129 us (33%)
  starting transfers between devices  66.9 us (17%)
  local copies, waits for them, and re-layouts  35 us (9%)
    ppermute x6, waiting for transfers between devices, turn(): lax.ppermute(block, axis, [(i, (i + step) % count) for i in range(count)])  77.6 us
    pallas_call x4, Pallas kernels, attention(): pl.pallas_call(partial(attention_kernel, q_count=q_count, columns_only=co...  48.9 us
    pallas_call x7, Pallas kernels, project(): pl.pallas_call(partial(project_kernel, count=len(pieces), carried=carry i...  44.3 us
    ppermute x30, waiting for transfers between devices, swap(): return lax.ppermute(block, axis, [(i, i ^ bit) for i in range(count)])  42 us
    ppermute x30, starting transfers between devices, swap(): return lax.ppermute(block, axis, [(i, i ^ bit) for i in range(count)])  39.7 us
    ppermute x8, waiting for transfers between devices, shift(): return lax.ppermute(block, axis, pairs)  35.6 us
    ppermute x8, starting transfers between devices, shift(): return lax.ppermute(block, axis, pairs)  20.6 us
    pallas_call x3, Pallas kernels, mix(): pl.pallas_call(mix_kernel, grid_spec=pltpu.PrefetchScalarGridSpec(num_sca...  17.4 us
  transfers between devices with their start and end apart: 44, of which 10 were waited for; matrix products, arithmetic and copies ran while one was open for 4% of the time, Pallas kernels for 31%

profile of v2, /device:TPU:17, one launch (start us, length us, event | category | flops | bytes accessed | tf_op | source)
XLA Modules:
  0.0 387.8 jit_solution(3991469730307205893)
XLA Ops:
  15.6 9.5 %collective-permute-done.8.refs_0_ = bf16[256,1280]{1,0:T(8,128)(2,1)} collective-permute-done((bf16[256,1280]{1,0:T(8,128)(2,1)S(1)}, bf16[256,1280]{1,0:T(8,128)(2,1)}, u32[]{:S(2)}, u32[]{:S(2)}) %collective-permute-start.8) | collective-permute-done | bytes 655392 | tf_op jit(solution)/shard_map/ppermute | solution.py:383
  27.2 18.9 %collective-permute-done.15.refs_0_ = bf16[384,1280]{1,0:T(8,128)(2,1)S(1)} collective-permute-done((bf16[384,1280]{1,0:T(8,128)(2,1)S(1)}, bf16[384,1280]{1,0:T(8,128)(2,1)S(1)}, u32[]{:S(2)}, u32[]{:S(2)}) %collective-permute-start.15) | collective-permute-done | bytes 983072 | tf_op jit(solution)/shard_map/ppermute | solution.py:383
  49.1 15.7 %collective-permute-done.1 = bf16[2,2,8,8,2560]{4,3,2,1,0:T(8,128)(2,1)S(1)} collective-permute-done((bf16[2,2,8,8,2560]{4,3,2,1,0:T(8,128)(2,1)}, bf16[2,2,8,8,2560]{4,3,2,1,0:T(8,128)(2,1)S(1)}, u32[]{:S(2)}, u32[]{:S(2)}) %collective-permute-start.1) | collective-permute-done | bytes 1310752 | tf_op jit(solution)/shard_map/ppermute | solution.py:378
  66.1 15.0 %collective-permute-start.38 = (bf16[384,1280]{1,0:T(8,128)(2,1)S(1)}, bf16[384,1280]{1,0:T(8,128)(2,1)}, u32[]{:S(2)}, u32[]{:S(2)}) collective-permute-start(bf16[384,1280]{1,0:T(8,128)(2,1)S(1)} %collective-permute-done.15.refs_0_), channel_id=1, source_target_pairs={{0,8},{8,0},{16,24},{24,16},{1,9},{9,1},{17,25},{25,17},{2,10},{10... | collective-permute-start | bytes 2949128 | tf_op jit(solution)/shard_map/ppermute | solution.py:388
  82.8 19.5 %collective-permute-done.9.refs_0_ = bf16[256,1280]{1,0:T(8,128)(2,1)S(1)} collective-permute-done((bf16[256,1280]{1,0:T(8,128)(2,1)}, bf16[256,1280]{1,0:T(8,128)(2,1)S(1)}, u32[]{:S(2)}, u32[]{:S(2)}) %collective-permute-start.9) | collective-permute-done | bytes 655392 | tf_op jit(solution)/shard_map/ppermute | solution.py:383
  117.1 29.8 %collective-permute-done.10.refs_0_ = bf16[256,1280]{1,0:T(8,128)(2,1)} collective-permute-done((bf16[256,1280]{1,0:T(8,128)(2,1)S(1)}, bf16[256,1280]{1,0:T(8,128)(2,1)}, u32[]{:S(2)}, u32[]{:S(2)}) %collective-permute-start.10) | collective-permute-done | bytes 655392 | tf_op jit(solution)/shard_map/ppermute | solution.py:383
  152.7 36.9 %collective-permute-done.40.refs_3_ = bf16[128,1280]{1,0:T(8,128)(2,1)} collective-permute-done((bf16[128,1280]{1,0:T(8,128)(2,1)}, bf16[128,1280]{1,0:T(8,128)(2,1)}, u32[]{:S(2)}, u32[]{:S(2)}) %collective-permute-start.40) | collective-permute-done | bytes 327712 | tf_op jit(solution)/shard_map/ppermute | solution.py:388
  190.9 12.6 %attend_neighbours.3 = (bf16[2,192,1408]{2,1,0:T(8,128)(2,1)S(1)}, bf16[2,192,1408]{2,1,0:T(8,128)(2,1)S(1)}) custom-call(s32[20,2]{1,0:T(8,128)S(1)} %copy.17.windows, s32[4]{0:T(128)S(1)} %add_convert_fusion.edges, bf16[2,192,2560]{2,1,0:T(8,128)(2,1)} %bitcast.72, bf16[2,192,2560]{2,1,0:T(8,128)(2,1)} %bitcast.74, bf16[2,2,192,2560]{3,2,1,0:T(8,128)(2,1)} %bitcast.68, ...), custom_call_target="tpu_custom_call" | custom-call | flops 1006632960 | bytes 20000000 | tf_op jit(solution)/shard_map/attend_neighbours/pallas_call | solution.py:138
  209.3 12.6 %attend_neighbours.2 = (bf16[2,192,1408]{2,1,0:T(8,128)(2,1)}, bf16[2,192,1408]{2,1,0:T(8,128)(2,1)}) custom-call(s32[20,2]{1,0:T(8,128)S(1)} %copy.17.windows, s32[4]{0:T(128)S(1)} %add_convert_fusion.edges, bf16[2,192,2560]{2,1,0:T(8,128)(2,1)} %bitcast.73, bf16[2,192,2560]{2,1,0:T(8,128)(2,1)} %bitcast.75, bf16[2,2,192,2560]{3,2,1,0:T(8,128)(2,1)} %bitcast.69, ...), custom_call_target="tpu_custom_call" | custom-call | flops 1006632960 | bytes 20000000 | tf_op jit(solution)/shard_map/attend_neighbours/pallas_call | solution.py:138
  243.1 13.5 %collective-permute-done.4.left.left_stat = bf16[2,192,1408]{2,1,0:T(8,128)(2,1)S(1)} collective-permute-done((bf16[2,192,1408]{2,1,0:T(8,128)(2,1)}, bf16[2,192,1408]{2,1,0:T(8,128)(2,1)S(1)}, u32[]{:S(2)}, u32[]{:S(2)}) %collective-permute-start.4) | collective-permute-done | bytes 1081376 | tf_op jit(solution)/shard_map/ppermute | solution.py:378
  264.0 11.8 %attend_own.3.own.own_stat = bf16[2,192,1408]{2,1,0:T(8,128)(2,1)S(1)} custom-call(s32[20,2]{1,0:T(8,128)S(1)} %copy.17.windows, s32[4]{0:T(128)S(1)} %add_convert_fusion.edges, bf16[2,192,2560]{2,1,0:T(8,128)(2,1)S(1)} %bitcast.66, bf16[2,2,192,2560]{3,2,1,0:T(8,128)(2,1)} %bitcast.70, bf16[2,2,64,2560]{3,2,1,0:T(8,128)(2,1)S(1)} %bitcast.60, ...), custom_call_target="tpu_custom_call" | custom-call | flops 503316480 | bytes 20000000 | tf_op jit(solution)/shard_map/attend_own/pallas_call | solution.py:138
  279.6 11.8 %attend_own.2.own.own_stat = bf16[2,192,1408]{2,1,0:T(8,128)(2,1)S(1)} custom-call(s32[20,2]{1,0:T(8,128)S(1)} %copy.17.windows, s32[4]{0:T(128)S(1)} %add_convert_fusion.edges, bf16[2,192,2560]{2,1,0:T(8,128)(2,1)S(1)} %bitcast.67, bf16[2,2,192,2560]{3,2,1,0:T(8,128)(2,1)} %bitcast.71, bf16[2,2,64,2560]{3,2,1,0:T(8,128)(2,1)S(1)} %bitcast.61, ...), custom_call_target="tpu_custom_call" | custom-call | flops 503316480 | bytes 20000000 | tf_op jit(solution)/shard_map/attend_own/pallas_call | solution.py:138
  297.9 6.9 %combine.3 = bf16[2,192,2560]{2,1,0:T(8,128)(2,1)S(1)} custom-call(s32[20,2]{1,0:T(8,128)S(1)} %copy.17.windows, s32[4]{0:T(128)S(1)} %add_convert_fusion.edges, bf16[2,192,1408]{2,1,0:T(8,128)(2,1)S(1)} %attend_own.2.own.own_stat, bf16[2,192,1408]{2,1,0:T(8,128)(2,1)S(1)} %copy-done.17, ...), custom_call_target="tpu_custom_call", output_to_operand_aliasing={{}: (8, {})} | custom-call | flops 4915200 | bytes 3932160 | tf_op jit(solution)/shard_map/combine/pallas_call | solution.py:202
  308.9 6.3 %project.11.refs_5_ = f32[384,1280]{1,0:T(8,128)S(1)} custom-call(s32[5]{0:T(128)S(1)} %stack.156.starts, bf16[384,2560]{1,0:T(8,128)(2,1)} %bitcast.46, bf16[384,1280]{1,0:T(8,128)(2,1)S(1)} %copy-done.27, bf16[384,1280]{1,0:T(8,128)(2,1)} %collective-permute-done.38.refs_1_, bf16[384,1280]{1,0:T(8,128)(2,1)S(1)} %copy-done.19, ...), custom_call_target="tpu_custom_call" | custom-call | flops 1509949440 | bytes 5898240 | tf_op jit(solution)/shard_map/project/pallas_call | solution.py:243
  316.2 6.4 %project.13.own_part = bf16[384,1280]{1,0:T(8,128)(2,1)S(1)} custom-call(s32[1]{0:T(128)} %constant.85.clone.1.starts, bf16[384,2560]{1,0:T(8,128)(2,1)S(1)} %bitcast.49, bf16[2560,1280]{1,0:T(8,128)(2,1)} %refs_0_.1), custom_call_target="tpu_custom_call" | custom-call | flops 2516582400 | bytes 8519680 | tf_op jit(solution)/shard_map/project/pallas_call | solution.py:243
  324.5 5.9 %project.12.own_part = bf16[384,1280]{1,0:T(8,128)(2,1)} custom-call(s32[5]{0:T(128)S(1)} %stack.145.starts, bf16[384,2560]{1,0:T(8,128)(2,1)S(1)} %bitcast.50, bf16[256,1280]{1,0:T(8,128)(2,1)} %collective-permute-done.8.refs_0_, bf16[256,1280]{1,0:T(8,128)(2,1)S(1)} %copy-done.23, bf16[256,1280]{1,0:T(8,128)(2,1)S(1)} %copy-done.21, ...), custom_call_target="tpu_custom_call" | custom-call | flops 1006632960 | bytes 4587520 | tf_op jit(solution)/shard_map/project/pallas_call | solution.py:243
  331.4 6.7 %project.9.refs_5_ = f32[384,1280]{1,0:T(8,128)S(1)} custom-call(s32[5]{0:T(128)S(1)} %stack.156.starts, bf16[384,2560]{1,0:T(8,128)(2,1)} %bitcast.47, bf16[384,1280]{1,0:T(8,128)(2,1)} %collective-permute-done.16.refs_0_, bf16[384,1280]{1,0:T(8,128)(2,1)} %collective-permute-done.29.refs_1_, bf16[384,1280]{1,0:T(8,128)(2,1)} %collective-permute-done.30.refs_2_, ...), custom_call_target="tpu_custom_call" | custom-call | flops 1509949440 | bytes 5898240 | tf_op jit(solution)/shard_map/project/pallas_call | solution.py:243
  339.4 6.3 %project.10.own_part = bf16[384,1280]{1,0:T(8,128)(2,1)} custom-call(s32[5]{0:T(128)S(1)} %stack.145.starts, bf16[384,2560]{1,0:T(8,128)(2,1)S(1)} %bitcast.51, bf16[256,1280]{1,0:T(8,128)(2,1)S(1)} %copy-done.29, bf16[256,1280]{1,0:T(8,128)(2,1)} %collective-permute-done.25.refs_1_, bf16[256,1280]{1,0:T(8,128)(2,1)} %collective-permute-done.26.refs_2_, ...), custom_call_target="tpu_custom_call" | custom-call | flops 1006632960 | bytes 4587520 | tf_op jit(solution)/shard_map/project/pallas_call | solution.py:243
  347.4 6.5 %project.7.refs_5_ = f32[384,1280]{1,0:T(8,128)S(1)} custom-call(s32[5]{0:T(128)S(1)} %stack.156.starts, bf16[384,2560]{1,0:T(8,128)(2,1)} %bitcast.48, bf16[384,1280]{1,0:T(8,128)(2,1)} %collective-permute-done.17.refs_0_, bf16[384,1280]{1,0:T(8,128)(2,1)} %collective-permute-done.18.refs_1_, bf16[384,1280]{1,0:T(8,128)(2,1)} %collective-permute-done.19.refs_2_, ...), custom_call_target="tpu_custom_call" | custom-call | flops 1509949440 | bytes 5898240 | tf_op jit(solution)/shard_map/project/pallas_call | solution.py:243
  355.7 6.2 %project.8.own_part = bf16[384,1280]{1,0:T(8,128)(2,1)} custom-call(s32[5]{0:T(128)S(1)} %stack.145.starts, bf16[384,2560]{1,0:T(8,128)(2,1)S(1)} %bitcast.52, bf16[256,1280]{1,0:T(8,128)(2,1)} %collective-permute-done.10.refs_0_, bf16[256,1280]{1,0:T(8,128)(2,1)} %collective-permute-done.11.refs_1_, bf16[256,1280]{1,0:T(8,128)(2,1)S(1)} %copy-done.25, ...), custom_call_target="tpu_custom_call" | custom-call | flops 1006632960 | bytes 4587520 | tf_op jit(solution)/shard_map/project/pallas_call | solution.py:243
  362.6 5.7 %mix.3 = (f32[384,3840]{1,0:T(8,128)}, f32[384,128]{1,0:T(8,128)S(1)}) custom-call(s32[3]{0:T(128)S(1)} %pad_add_fusion.3.place, bf16[384,1280]{1,0:T(8,128)(2,1)S(1)} %project.13.own_part, bf16[384,1280]{1,0:T(8,128)(2,1)} %collective-permute-done.43.other_part, bf16[384,2560]{1,0:T(8,128)(2,1)S(1)} %bitcast.54, ...), custom_call_target="tpu_custom_call" | custom-call | flops 4915200 | bytes 5898240 | tf_op jit(solution)/shard_map/mix/pallas_call | solution.py:294
  368.3 5.8 %mix.4 = (f32[384,3840]{1,0:T(8,128)}, f32[384,128]{1,0:T(8,128)S(1)}) custom-call(s32[3]{0:T(128)S(1)} %pad_add_fusion.2.place, bf16[384,1280]{1,0:T(8,128)(2,1)} %project.12.own_part, bf16[384,1280]{1,0:T(8,128)(2,1)} %collective-permute-done.42.other_part, bf16[384,2560]{1,0:T(8,128)(2,1)S(1)} %bitcast.55, ...), custom_call_target="tpu_custom_call", output_to_operand_aliasing={{0}: (8, {})} | custom-call | flops 4915200 | bytes 5898240 | tf_op jit(solution)/shard_map/mix/pallas_call | solution.py:294
  374.1 5.8 %mix.5 = (f32[384,3840]{1,0:T(8,128)}, f32[384,128]{1,0:T(8,128)S(1)}) custom-call(s32[3]{0:T(128)S(1)} %pad_add_fusion.1.place, bf16[384,1280]{1,0:T(8,128)(2,1)} %project.10.own_part, bf16[384,1280]{1,0:T(8,128)(2,1)} %collective-permute-done.33.other_part, bf16[384,2560]{1,0:T(8,128)(2,1)S(1)} %bitcast.56, ...), custom_call_target="tpu_custom_call", output_to_operand_aliasing={{0}: (8, {})} | custom-call | flops 4915200 | bytes 5898240 | tf_op jit(solution)/shard_map/mix/pallas_call | solution.py:294
  380.0 7.9 %finish.1 = (bf16[384,2560]{1,0:T(8,128)(2,1)}, bf16[384,2560]{1,0:T(8,128)(2,1)}) custom-call(s32[3]{0:T(128)S(1)} %pad_add_fusion.place, bf16[384,1280]{1,0:T(8,128)(2,1)} %project.8.own_part, bf16[384,1280]{1,0:T(8,128)(2,1)} %collective-permute-done.22.other_part, bf16[384,2560]{1,0:T(8,128)(2,1)S(1)} %bitcast.57, ...), custom_call_target="tpu_custom_call" | custom-call | flops 19660800 | bytes 11796480 | tf_op jit(solution)/shard_map/finish/pallas_call | solution.py:355
  (179 shorter events, 102.0 us)
Async XLA Ops:
  4.0 44.7 %collective-permute-start = (bf16[2,2,8,8,2560]{4,3,2,1,0:T(8,128)(2,1)}, bf16[2,2,8,8,2560]{4,3,2,1,0:T(8,128)(2,1)S(1)}, u32[]{:S(2)}, u32[]{:S(2)}) collective-permute-start(bf16[2,2,8,8,2560]{4,3,2,1,0:T(8,128)(2,1)} %get-tuple-element.27), channel_id=1, source_target_pairs={{0,8},{8,16},{16,24},{1,9},{9,17},{17,25},{2,10},{10,18},{18,26},{... | collective-permute-start | bytes 3932168 | tf_op jit(solution)/shard_map/ppermute | solution.py:378
  7.2 57.6 %collective-permute-start.1 = (bf16[2,2,8,8,2560]{4,3,2,1,0:T(8,128)(2,1)}, bf16[2,2,8,8,2560]{4,3,2,1,0:T(8,128)(2,1)S(1)}, u32[]{:S(2)}, u32[]{:S(2)}) collective-permute-start(bf16[2,2,8,8,2560]{4,3,2,1,0:T(8,128)(2,1)} %get-tuple-element.26), channel_id=1, source_target_pairs={{8,0},{16,8},{24,16},{9,1},{17,9},{25,17},{10,2},{18,10},{26,18},{... | collective-permute-start | bytes 3932168 | tf_op jit(solution)/shard_map/ppermute | solution.py:378
  12.8 100.8 %collective-permute-start.2 = (bf16[2,24,8,2560]{3,2,1,0:T(8,128)(2,1)S(1)}, bf16[2,24,8,2560]{3,2,1,0:T(8,128)(2,1)S(1)}, u32[]{:S(2)}, u32[]{:S(2)}) collective-permute-start(bf16[2,24,8,2560]{3,2,1,0:T(8,128)(2,1)S(1)} %copy-done.7), channel_id=1, source_target_pairs={{0,2},{2,4},{4,6},{1,3},{3,5},{5,7},{8,10},{10,12},{12,14},{9,11},... | collective-permute-start | bytes 5898248 | tf_op jit(solution)/shard_map/ppermute | solution.py:378
  25.1 89.8 %collective-permute-start.3 = (bf16[2,24,8,2560]{3,2,1,0:T(8,128)(2,1)S(1)}, bf16[2,24,8,2560]{3,2,1,0:T(8,128)(2,1)S(1)}, u32[]{:S(2)}, u32[]{:S(2)}) collective-permute-start(bf16[2,24,8,2560]{3,2,1,0:T(8,128)(2,1)S(1)} %copy-done.7), channel_id=1, source_target_pairs={{2,0},{4,2},{6,4},{3,1},{5,3},{7,5},{10,8},{12,10},{14,12},{11,9},... | collective-permute-start | bytes 5898248 | tf_op jit(solution)/shard_map/ppermute | solution.py:378
  64.8 37.5 %collective-permute-start.9 = (bf16[256,1280]{1,0:T(8,128)(2,1)}, bf16[256,1280]{1,0:T(8,128)(2,1)S(1)}, u32[]{:S(2)}, u32[]{:S(2)}) collective-permute-start(bf16[256,1280]{1,0:T(8,128)(2,1)} %collective-permute-done.8.refs_0_), channel_id=1, source_target_pairs={{0,2},{2,4},{4,6},{6,0},{1,3},{3,5},{5,7},{7,1},{8,10},{10,12},{12... | collective-permute-start | bytes 1966088 | tf_op jit(solution)/shard_map/ppermute | solution.py:383
  66.1 49.1 %collective-permute-start.38 = (bf16[384,1280]{1,0:T(8,128)(2,1)S(1)}, bf16[384,1280]{1,0:T(8,128)(2,1)}, u32[]{:S(2)}, u32[]{:S(2)}) collective-permute-start(bf16[384,1280]{1,0:T(8,128)(2,1)S(1)} %collective-permute-done.15.refs_0_), channel_id=1, source_target_pairs={{0,8},{8,0},{16,24},{24,16},{1,9},{9,1},{17,25},{25,17},{2,10},{10... | collective-permute-start | bytes 2949128 | tf_op jit(solution)/shard_map/ppermute | solution.py:388
  110.5 36.4 %collective-permute-start.16 = (bf16[384,1280]{1,0:T(8,128)(2,1)S(1)}, bf16[384,1280]{1,0:T(8,128)(2,1)}, u32[]{:S(2)}, u32[]{:S(2)}) collective-permute-start(bf16[384,1280]{1,0:T(8,128)(2,1)S(1)} %collective-permute-done.15.refs_0_), channel_id=1, source_target_pairs={{0,2},{2,4},{4,6},{6,0},{1,3},{3,5},{5,7},{7,1},{8,10},{10,12},{12... | collective-permute-start | bytes 2949128 | tf_op jit(solution)/shard_map/ppermute | solution.py:383
  112.6 35.2 %collective-permute-start.39 = (bf16[384,1280]{1,0:T(8,128)(2,1)S(1)}, bf16[384,1280]{1,0:T(8,128)(2,1)S(1)}, u32[]{:S(2)}, u32[]{:S(2)}) collective-permute-start(bf16[384,1280]{1,0:T(8,128)(2,1)S(1)} %collective-permute-done.15.refs_0_), channel_id=1, source_target_pairs={{0,16},{8,24},{16,0},{24,8},{1,17},{9,25},{17,1},{25,9},{2,18},{10... | collective-permute-start | bytes 2949128 | tf_op jit(solution)/shard_map/ppermute | solution.py:388
  114.9 34.3 %collective-permute-start.26 = (bf16[256,1280]{1,0:T(8,128)(2,1)S(1)}, bf16[256,1280]{1,0:T(8,128)(2,1)}, u32[]{:S(2)}, u32[]{:S(2)}) collective-permute-start(bf16[256,1280]{1,0:T(8,128)(2,1)S(1)} %collective-permute-done.9.refs_0_), channel_id=1, source_target_pairs={{0,16},{8,24},{16,0},{24,8},{1,17},{9,25},{17,1},{25,9},{2,18},{10... | collective-permute-start | bytes 1966088 | tf_op jit(solution)/shard_map/ppermute | solution.py:388
  115.2 36.4 %collective-permute-start.25 = (bf16[256,1280]{1,0:T(8,128)(2,1)S(1)}, bf16[256,1280]{1,0:T(8,128)(2,1)}, u32[]{:S(2)}, u32[]{:S(2)}) collective-permute-start(bf16[256,1280]{1,0:T(8,128)(2,1)S(1)} %collective-permute-done.9.refs_0_), channel_id=1, source_target_pairs={{0,8},{8,0},{16,24},{24,16},{1,9},{9,1},{17,25},{25,17},{2,10},{10... | collective-permute-start | bytes 1966088 | tf_op jit(solution)/shard_map/ppermute | solution.py:388
  146.9 56.6 %collective-permute-start.12 = (bf16[256,1280]{1,0:T(8,128)(2,1)}, bf16[256,1280]{1,0:T(8,128)(2,1)S(1)}, u32[]{:S(2)}, u32[]{:S(2)}) collective-permute-start(bf16[256,1280]{1,0:T(8,128)(2,1)} %collective-permute-done.10.refs_0_), channel_id=1, source_target_pairs={{0,16},{8,24},{16,0},{24,8},{1,17},{9,25},{17,1},{25,9},{2,18},{10... | collective-permute-start | bytes 1966088 | tf_op jit(solution)/shard_map/ppermute | solution.py:388
  146.9 75.1 %collective-permute-start.29 = (bf16[384,1280]{1,0:T(8,128)(2,1)}, bf16[384,1280]{1,0:T(8,128)(2,1)}, u32[]{:S(2)}, u32[]{:S(2)}) collective-permute-start(bf16[384,1280]{1,0:T(8,128)(2,1)} %collective-permute-done.16.refs_0_), channel_id=1, source_target_pairs={{0,8},{8,0},{16,24},{24,16},{1,9},{9,1},{17,25},{25,17},{2,10},{10... | collective-permute-start | bytes 2949128 | tf_op jit(solution)/shard_map/ppermute | solution.py:388
  147.7 77.7 %collective-permute-start.30 = (bf16[384,1280]{1,0:T(8,128)(2,1)}, bf16[384,1280]{1,0:T(8,128)(2,1)}, u32[]{:S(2)}, u32[]{:S(2)}) collective-permute-start(bf16[384,1280]{1,0:T(8,128)(2,1)} %collective-permute-done.16.refs_0_), channel_id=1, source_target_pairs={{0,16},{8,24},{16,0},{24,8},{1,17},{9,25},{17,1},{25,9},{2,18},{10... | collective-permute-start | bytes 2949128 | tf_op jit(solution)/shard_map/ppermute | solution.py:388
  149.2 58.2 %collective-permute-start.11 = (bf16[256,1280]{1,0:T(8,128)(2,1)}, bf16[256,1280]{1,0:T(8,128)(2,1)}, u32[]{:S(2)}, u32[]{:S(2)}) collective-permute-start(bf16[256,1280]{1,0:T(8,128)(2,1)} %collective-permute-done.10.refs_0_), channel_id=1, source_target_pairs={{0,8},{8,0},{16,24},{24,16},{1,9},{9,1},{17,25},{25,17},{2,10},{10... | collective-permute-start | bytes 1966088 | tf_op jit(solution)/shard_map/ppermute | solution.py:388
  151.6 38.0 %collective-permute-start.40 = (bf16[128,1280]{1,0:T(8,128)(2,1)}, bf16[128,1280]{1,0:T(8,128)(2,1)}, u32[]{:S(2)}, u32[]{:S(2)}) collective-permute-start(bf16[128,1280]{1,0:T(8,128)(2,1)} %slice.90), channel_id=1, source_target_pairs={{0,8},{8,0},{16,24},{24,16},{1,9},{9,1},{17,25},{25,17},{2,10},{10... | collective-permute-start | bytes 983048 | tf_op jit(solution)/shard_map/ppermute | solution.py:388
  189.6 37.9 %collective-permute-start.17 = (bf16[384,1280]{1,0:T(8,128)(2,1)}, bf16[384,1280]{1,0:T(8,128)(2,1)}, u32[]{:S(2)}, u32[]{:S(2)}) collective-permute-start(bf16[384,1280]{1,0:T(8,128)(2,1)} %collective-permute-done.16.refs_0_), channel_id=1, source_target_pairs={{0,2},{2,4},{4,6},{6,0},{1,3},{3,5},{5,7},{7,1},{8,10},{10,12},{12... | collective-permute-start | bytes 2949128 | tf_op jit(solution)/shard_map/ppermute | solution.py:383
  222.0 34.7 %collective-permute-start.4 = (bf16[2,192,1408]{2,1,0:T(8,128)(2,1)}, bf16[2,192,1408]{2,1,0:T(8,128)(2,1)S(1)}, u32[]{:S(2)}, u32[]{:S(2)}) collective-permute-start(bf16[2,192,1408]{2,1,0:T(8,128)(2,1)} %get-tuple-element.14), channel_id=1, source_target_pairs={{0,2},{2,4},{4,6},{1,3},{3,5},{5,7},{8,10},{10,12},{12,14},{9,11},... | collective-permute-start | bytes 3244040 | tf_op jit(solution)/shard_map/ppermute | solution.py:378
  227.6 48.3 %collective-permute-start.18 = (bf16[384,1280]{1,0:T(8,128)(2,1)}, bf16[384,1280]{1,0:T(8,128)(2,1)}, u32[]{:S(2)}, u32[]{:S(2)}) collective-permute-start(bf16[384,1280]{1,0:T(8,128)(2,1)} %collective-permute-done.17.refs_0_), channel_id=1, source_target_pairs={{0,8},{8,0},{16,24},{24,16},{1,9},{9,1},{17,25},{25,17},{2,10},{10... | collective-permute-start | bytes 2949128 | tf_op jit(solution)/shard_map/ppermute | solution.py:388
  234.3 80.9 %collective-permute-start.19 = (bf16[384,1280]{1,0:T(8,128)(2,1)}, bf16[384,1280]{1,0:T(8,128)(2,1)}, u32[]{:S(2)}, u32[]{:S(2)}) collective-permute-start(bf16[384,1280]{1,0:T(8,128)(2,1)} %collective-permute-done.17.refs_0_), channel_id=1, source_target_pairs={{0,16},{8,24},{16,0},{24,8},{1,17},{9,25},{17,1},{25,9},{2,18},{10... | collective-permute-start | bytes 2949128 | tf_op jit(solution)/shard_map/ppermute | solution.py:388
  238.2 69.5 %collective-permute-start.41 = (bf16[256,1280]{1,0:T(8,128)(2,1)}, bf16[256,1280]{1,0:T(8,128)(2,1)}, u32[]{:S(2)}, u32[]{:S(2)}) collective-permute-start(bf16[256,1280]{1,0:T(8,128)(2,1)} %slice.91), channel_id=1, source_target_pairs={{0,16},{8,24},{16,0},{24,8},{1,17},{9,25},{17,1},{25,9},{2,18},{10... | collective-permute-start | bytes 1966088 | tf_op jit(solution)/shard_map/ppermute | solution.py:388
  257.6 49.7 %collective-permute-start.27 = (bf16[128,1280]{1,0:T(8,128)(2,1)}, bf16[128,1280]{1,0:T(8,128)(2,1)}, u32[]{:S(2)}, u32[]{:S(2)}) collective-permute-start(bf16[128,1280]{1,0:T(8,128)(2,1)} %slice.84), channel_id=1, source_target_pairs={{0,8},{8,0},{16,24},{24,16},{1,9},{9,1},{17,25},{25,17},{2,10},{10... | collective-permute-start | bytes 983048 | tf_op jit(solution)/shard_map/ppermute | solution.py:388
  258.9 72.3 %collective-permute-start.32 = (bf16[256,1280]{1,0:T(8,128)(2,1)}, bf16[256,1280]{1,0:T(8,128)(2,1)}, u32[]{:S(2)}, u32[]{:S(2)}) collective-permute-start(bf16[256,1280]{1,0:T(8,128)(2,1)} %slice.87), channel_id=1, source_target_pairs={{0,16},{8,24},{16,0},{24,8},{1,17},{9,25},{17,1},{25,9},{2,18},{10... | collective-permute-start | bytes 1966088 | tf_op jit(solution)/shard_map/ppermute | solution.py:388
  275.8 86.8 %collective-permute-start.23 = (bf16[384,2560]{1,0:T(8,128)(2,1)S(1)}, bf16[384,2560]{1,0:T(8,128)(2,1)}, u32[]{:S(2)}, u32[]{:S(2)}) collective-permute-start(bf16[384,2560]{1,0:T(8,128)(2,1)S(1)} %bitcast.53), channel_id=1, source_target_pairs={{0,1},{1,0},{2,3},{3,2},{4,5},{5,4},{6,7},{7,6},{8,9},{9,8},{10,11... | collective-permute-start | bytes 5898248 | tf_op jit(solution)/shard_map/ppermute | solution.py:388
  307.7 39.6 %collective-permute-start.21 = (bf16[256,1280]{1,0:T(8,128)(2,1)S(1)}, bf16[256,1280]{1,0:T(8,128)(2,1)S(1)}, u32[]{:S(2)}, u32[]{:S(2)}) collective-permute-start(bf16[256,1280]{1,0:T(8,128)(2,1)S(1)} %slice.83), channel_id=1, source_target_pairs={{0,16},{8,24},{16,0},{24,8},{1,17},{9,25},{17,1},{25,9},{2,18},{10... | collective-permute-start | bytes 1966088 | tf_op jit(solution)/shard_map/ppermute | solution.py:388
  (57 other events, 978.4 us)

commit v3 on v2

--- a/solution.py
+++ b/solution.py
@@ -16,7 +16,7 @@
 
 EPSILON = 1e-06
 VMEM_LIMIT = 48 * 1024 * 1024
-HEAD_GROUPS = 2
+SMALL = pl.CostEstimate(flops=1, bytes_accessed=1, transcendentals=0)
 
 
 def kernel_params():
@@ -25,11 +25,11 @@
     )
 
 
-def attention_kernel(windows, edges, *refs, q_count, columns_only, first_head, group):
+def attention_kernel(windows, edges, *refs, q_count, columns_only, first_head, group, waits):
     q_refs = refs[:q_count]
     kv_ref, top_ref, bottom_ref = refs[q_count : q_count + 3]
-    out_refs = refs[q_count + 3 : 2 * q_count + 3]
-    stat_refs = refs[2 * q_count + 3 :]
+    refs = refs[q_count + 3 + waits :]
+    out_refs, stat_refs = refs[:q_count], refs[q_count:]
     frames, tokens, head_size = q_refs[0].shape
     span = top_ref.shape[2]
     tiles = tokens // span
@@ -121,7 +121,7 @@
             out_ref[...] = packed.astype(jnp.bfloat16)
 
 
-def attention(windows, edges, query_blocks, keys_values, top, bottom, columns_only, first_head, group):
+def attention(windows, edges, query_blocks, keys_values, top, bottom, columns_only, first_head, group, after):
     frames, tokens, features = query_blocks[0].shape
     head_size = features // windows.shape[0]
     span = top.shape[2]
@@ -134,7 +134,6 @@
     kv_spec = pl.BlockSpec((2, frames, tokens, head_size), lambda h, *_: (0, 0, 0, head_of(h)))
     halo_spec = pl.BlockSpec((2, frames, span, head_size), lambda h, *_: (0, 0, 0, head_of(h)))
     out_spec = pl.BlockSpec((frames, tokens, head_size), lambda h, *_: (0, 0, h))
-    flops = 4 * q_count * frames * tokens * 2 * frames * span * head_size * group
     return pl.pallas_call(
         partial(
             attention_kernel,
@@ -142,22 +141,22 @@
             columns_only=columns_only,
             first_head=first_head,
             group=group,
+            waits=len(after),
         ),
         grid_spec=pltpu.PrefetchScalarGridSpec(
             num_scalar_prefetch=2,
             grid=(group + 1,),
-            in_specs=[q_spec] * q_count + [kv_spec, halo_spec, halo_spec],
+            in_specs=[q_spec] * q_count + [kv_spec, halo_spec, halo_spec]
+            + [pl.BlockSpec(memory_space=pl.ANY)] * len(after),
             out_specs=[out_spec] * q_count,
             scratch_shapes=[pltpu.VMEM((frames, tokens, LANES), jnp.float32)] * q_count,
         ),
         out_shape=[jax.ShapeDtypeStruct((frames, tokens, (group + 1) * head_size), jnp.bfloat16)]
         * q_count,
         compiler_params=kernel_params(),
-        cost_estimate=pl.CostEstimate(
-            flops=flops, bytes_accessed=20_000_000, transcendentals=flops // 256
-        ),
+        cost_estimate=SMALL,
         name="attend_neighbours" if columns_only else "attend_own",
-    )(windows, edges, *query_blocks, keys_values, top, bottom)
+    )(windows, edges, *query_blocks, keys_values, top, bottom, *after)
 
 
 def combine_kernel(windows, edges, own, left, right, own_stat, left_stat, right_stat, *rest, first_head):
@@ -193,40 +192,41 @@
         out[...] = (mixed / (weights[0] + weights[1] + weights[2])).astype(jnp.bfloat16)
 
 
-def combine(windows, edges, outputs, first_head, group, features, so_far):
+def combine(windows, edges, outputs, first_head, group, features, so_far, order):
     frames, tokens, _ = outputs[0].shape
     head_size = features // windows.shape[0]
     spec = pl.BlockSpec((frames, tokens, head_size), lambda h, *_: (0, 0, h))
     stat_spec = pl.BlockSpec((frames, tokens, head_size), lambda h, *_: (0, 0, group))
     more = [] if so_far is None else [so_far]
+    share = windows.shape[0] // order
+
+    def out_index(h, windows, edges):
+        head = first_head + h
+        return 0, 0, ((head // share) ^ edges[4]) * share + lax.rem(head, share)
+
     return pl.pallas_call(
         partial(combine_kernel, first_head=first_head),
         grid_spec=pltpu.PrefetchScalarGridSpec(
             num_scalar_prefetch=2,
             grid=(group,),
             in_specs=[spec] * 3 + [stat_spec] * 3 + [pl.BlockSpec(memory_space=pl.ANY)] * len(more),
-            out_specs=pl.BlockSpec((frames, tokens, head_size), lambda h, *_: (0, 0, first_head + h)),
+            out_specs=pl.BlockSpec((frames, tokens, head_size), out_index),
         ),
         out_shape=jax.ShapeDtypeStruct((frames, tokens, features), jnp.bfloat16),
         input_output_aliases={8: 0} if more else {},
         compiler_params=kernel_params(),
-        cost_estimate=pl.CostEstimate(
-            flops=10 * frames * tokens * head_size * group,
-            bytes_accessed=8 * frames * tokens * head_size * group,
-            transcendentals=0,
-        ),
+        cost_estimate=SMALL,
         name="combine",
     )(windows, edges, *outputs, *outputs, *more)
 
 
-def project_kernel(starts, attended, *refs, count, carried):
-    pieces = refs[:count]
+def project_kernel(place, attended, *refs, offsets, carried):
+    pieces = refs[: len(offsets)]
     out = refs[-1]
-    total = refs[count][...] if carried else None
-    for index, piece in enumerate(pieces):
-        start = pl.multiple_of(starts[index], LANES)
+    total = refs[len(offsets)][...] if carried else None
+    for piece, offset in zip(pieces, offsets):
         term = jnp.dot(
-            attended[:, pl.ds(start, piece.shape[0])],
+            attended[:, offset : offset + piece.shape[0]],
             piece[...],
             preferred_element_type=jnp.float32,
         )
@@ -234,31 +234,32 @@
     out[...] = total.astype(out.dtype)
 
 
-def project(attended, pieces, starts, carry, dtype):
+def project(place, attended, pieces, carry, dtype):
     tokens, features = attended.shape
-    width = pieces[0].shape[1]
-    column = 256 if width % 256 == 0 else width
-    depth = sum(piece.shape[0] for piece in pieces)
+    width = pieces[0][0].shape[1]
+    column = 640 if width % 640 == 0 else width
     out_spec = pl.BlockSpec((tokens, column), lambda i, _: (0, i))
+    piece_specs = [
+        pl.BlockSpec((rows, column), lambda i, place, block=block: (block(place), i))
+        for _, rows, block, _ in pieces
+    ]
     return pl.pallas_call(
-        partial(project_kernel, count=len(pieces), carried=carry is not None),
+        partial(
+            project_kernel, offsets=[piece[3] for piece in pieces], carried=carry is not None
+        ),
         grid_spec=pltpu.PrefetchScalarGridSpec(
             num_scalar_prefetch=1,
             grid=(width // column,),
             in_specs=[pl.BlockSpec((tokens, features), lambda i, _: (0, 0))]
-            + [pl.BlockSpec((piece.shape[0], column), lambda i, _: (0, i)) for piece in pieces]
+            + piece_specs
             + ([] if carry is None else [out_spec]),
             out_specs=out_spec,
         ),
         out_shape=jax.ShapeDtypeStruct((tokens, width), dtype),
         compiler_params=kernel_params(),
-        cost_estimate=pl.CostEstimate(
-            flops=2 * tokens * depth * width,
-            bytes_accessed=2 * depth * width + 2 * tokens * features,
-            transcendentals=0,
-        ),
+        cost_estimate=SMALL,
         name="project",
-    )(jnp.stack(starts).astype(jnp.int32), attended, *pieces, *([] if carry is None else [carry]))
+    )(place, attended, *[piece[0] for piece in pieces], *([] if carry is None else [carry]))
 
 
 def mix_kernel(place, own_part, other_part, own_hidden, other_hidden, own_gate, other_gate, *refs):
@@ -284,7 +285,7 @@
 def mix(place, own_part, other_part, own_hidden, other_hidden, own_gate, other_gate, carry):
     tokens, width = own_part.shape
     blocks = own_hidden.shape[1] // width
-    rows = 64 if tokens % 64 == 0 else tokens
+    rows = 128 if tokens % 128 == 0 else tokens
     part = pl.BlockSpec((rows, width), lambda i, place: (i, 0))
     hidden = pl.BlockSpec((rows, width), lambda i, place: (i, place[1]))
     gate = pl.BlockSpec((1, width), lambda i, place: (0, place[1]))
@@ -306,9 +307,7 @@
         ],
         input_output_aliases={8: 0} if more else {},
         compiler_params=kernel_params(),
-        cost_estimate=pl.CostEstimate(
-            flops=10 * tokens * width, bytes_accessed=12 * tokens * width, transcendentals=0
-        ),
+        cost_estimate=SMALL,
         name="mix",
     )(place, own_part, other_part, own_hidden, other_hidden, own_gate, other_gate, *more)
 
@@ -345,7 +344,7 @@
 def finish(place, own_part, other_part, own_hidden, other_hidden, own_gate, other_gate, scale, shift_by, carry):
     tokens, width = own_part.shape
     features = own_hidden.shape[1]
-    rows = 64 if tokens % 64 == 0 else tokens
+    rows = 128 if tokens % 128 == 0 else tokens
     part = pl.BlockSpec((rows, width), lambda i, place: (i, 0))
     hidden = pl.BlockSpec((rows, width), lambda i, place: (i, place[1]))
     gate = pl.BlockSpec((1, width), lambda i, place: (0, place[1]))
@@ -362,9 +361,7 @@
         ),
         out_shape=[jax.ShapeDtypeStruct((tokens, features), jnp.bfloat16)] * 2,
         compiler_params=kernel_params(),
-        cost_estimate=pl.CostEstimate(
-            flops=20 * tokens * features, bytes_accessed=12 * tokens * features, transcendentals=0
-        ),
+        cost_estimate=SMALL,
         name="finish",
     )(
         place, own_part, other_part, own_hidden, other_hidden, own_gate, other_gate, scale,
@@ -388,93 +385,152 @@
     return lax.ppermute(block, axis, [(i, i ^ bit) for i in range(count)])
 
 
-def attend_all(queries, keys_values, windows):
-    frames, rows, cols, features = queries.shape
-    n_ha, n_wa = lax.axis_size("ha"), lax.axis_size("wa")
-    ha, wa = lax.axis_index("ha"), lax.axis_index("wa")
-    head_count = windows.shape[0]
-
-    edges = jnp.stack([ha > 0, ha < n_ha - 1, wa > 0, wa < n_wa - 1]).astype(jnp.int32)
-    from_left = shift(queries, "wa", 1)
-    from_right = shift(queries, "wa", -1)
-    top = shift(keys_values[:, :, rows - TILE :], "ha", 1)
-    bottom = shift(keys_values[:, :, :TILE], "ha", -1)
-
-    def flat(block):
-        return block.reshape(block.shape[:-3] + (-1, features))
-
-    held = flat(keys_values), flat(top), flat(bottom)
-    groups = HEAD_GROUPS if head_count % HEAD_GROUPS == 0 else 1
-    group = head_count // groups
-    far = []
-    for first in range(0, head_count, group):
-        for_left, for_right = attention(
-            windows, edges, [flat(from_left), flat(from_right)], *held, True, first, group
+class Tokens:
+    def __init__(self, queries, keys_values, windows, order):
+        rows = queries.shape[1]
+        features = queries.shape[3]
+        n_ha, n_wa = lax.axis_size("ha"), lax.axis_size("wa")
+        ha, wa = lax.axis_index("ha"), lax.axis_index("wa")
+
+        def flat(block):
+            return block.reshape(block.shape[:-3] + (-1, features))
+
+        turned = ha if order > 1 else 0 * ha
+        self.edges = jnp.stack([ha > 0, ha < n_ha - 1, wa > 0, wa < n_wa - 1, turned]).astype(
+            jnp.int32
         )
-        far.append((shift(for_right, "wa", 1), shift(for_left, "wa", -1)))
-    near = [
-        attention(windows, edges, [flat(queries)], *held, False, first, group)[0]
-        for first in range(0, head_count, group)
+        self.windows = windows
+        self.order = order
+        self.features = features
+        self.queries = flat(queries)
+        self.keys_values = flat(keys_values)
+        last, first = lax.optimization_barrier(
+            (keys_values[:, :, rows - TILE :], keys_values[:, :, :TILE])
+        )
+        self.halos = [flat(shift(last, "ha", 1)), flat(shift(first, "ha", -1))]
+        self.visitors = [flat(shift(queries, "wa", 1)), flat(shift(queries, "wa", -1))]
+
+    def attend(self, query_blocks, columns_only):
+        return attention(
+            self.windows,
+            self.edges,
+            query_blocks,
+            self.keys_values,
+            *self.halos,
+            columns_only,
+            0,
+            self.windows.shape[0],
+            [],
+        )
+
+    def stay(self):
+        self.near = self.attend([self.queries], False)
+
+    def visit(self):
+        self.ends = self.attend(self.visitors, True)
+
+    def send_back(self):
+        for_left, for_right = self.ends
+        self.back = [shift(for_right, "wa", 1), shift(for_left, "wa", -1)]
+
+    def combine(self):
+        attended = combine(
+            self.windows,
+            self.edges,
+            [*self.near, *self.back],
+            0,
+            self.windows.shape[0],
+            self.features,
+            None,
+            self.order,
+        )
+        return attended.reshape(-1, self.features)
+
+
+def together(*groups):
+    blocks = iter(lax.optimization_barrier(tuple(block for group in groups for block in group)))
+    return [[next(blocks) for _ in group] for group in groups]
+
+
+def paired(hidden, queries, keys_values, windows, out_weight, picked):
+    ha, wa, ta = lax.axis_index("ha"), lax.axis_index("wa"), lax.axis_index("ta")
+    n_wa = lax.axis_size("wa")
+    blocks = n_wa // 2
+    depth = out_weight.shape[0] // 4
+    cut = depth * 2 // 5
+
+    def swaps(share):
+        return [swap(share, "ha", 1), swap(share, "ha", 2)]
+
+    def far_swaps(by_x, by_y):
+        return [swap(by_y[:cut], "ha", 1), swap(by_x[cut:], "ha", 2)]
+
+    share = lax.optimization_barrier(lax.dynamic_slice_in_dim(out_weight, ha * depth, depth, 0))
+    first = turn(share, "wa", 1)
+    tokens = Tokens(queries, keys_values, windows, 4)
+
+    [first], tokens.halos = together([first], tokens.halos)
+    first_near = swaps(first)
+    second = turn(first, "wa", 1)
+    tokens.stay()
+
+    first_near, tokens.near, tokens.visitors = together(first_near, tokens.near, tokens.visitors)
+    first_far = far_swaps(*first_near)
+    tokens.visit()
+
+    [second], first_far, tokens.ends = together([second], first_far, tokens.ends)
+    third = turn(second, "wa", 1)
+    second_near = swaps(second)
+    tokens.send_back()
+
+    [third], second_near = together([third], second_near)
+    third_near = swaps(third)
+    second_far = far_swaps(*second_near)
+
+    tokens.back, second_far = together(tokens.back, second_far)
+    attended = tokens.combine()
+
+    third_near, [attended] = together(third_near, [attended])
+    third_far = far_swaps(*third_near)
+    slots = [
+        [first, *first_near, *first_far],
+        [second, *second_near, *second_far],
+        [third, *third_near, *third_far],
     ]
-    attended = None
-    for index, first in enumerate(range(0, head_count, group)):
-        attended = combine(
-            windows, edges, [near[index], *far[index]], first, group, features, attended
-        )
-    return attended.reshape(-1, features)
-
-
-def gather_slots(out_weight):
-    n_wa = lax.axis_size("wa")
-    ha = lax.axis_index("ha")
-    depth = out_weight.shape[0] // lax.axis_size("ha")
-    half = max(depth * 3 // 5 // LANES, 1) * LANES
-    cuts = [(0, half), (half, depth)] if half < depth else [(0, depth)]
-    held = [
-        lax.dynamic_slice_in_dim(out_weight, ha * depth + low, high - low, 0) for low, high in cuts
-    ]
-    slots = []
-    for _ in range(1, n_wa):
-        slot = []
-        for index, (low, high) in enumerate(cuts):
-            held[index] = turn(held[index], "wa", 1)
-            mine = held[index]
-            by_x = swap(mine, "ha", 1)
-            by_y = swap(mine, "ha", 2)
-            split = LANES if high - low > LANES else (high - low) // 2
-            far_x = swap(by_y[:split], "ha", 1)
-            far_y = swap(by_x[split:], "ha", 2)
-            slot.append(
-                [
-                    (mine, ha * depth + low),
-                    (by_x, (ha ^ 1) * depth + low),
-                    (by_y, (ha ^ 2) * depth + low),
-                    (far_x, (ha ^ 3) * depth + low),
-                    (far_y, (ha ^ 3) * depth + low + split),
-                ]
-            )
-        slots.append(slot)
-    return slots
-
-
-def paired(hidden, attended, out_weight, picked):
-    n_wa = lax.axis_size("wa")
-    wa, ta = lax.axis_index("wa"), lax.axis_index("ta")
-    blocks = n_wa // 2
+
     other_hidden = swap(hidden, "ta", 1)
     gate = picked[0:1]
     other_gate = swap(gate, "ta", 1)
-    slots = [[[(out_weight, jnp.int32(0))]]] + gather_slots(out_weight)
+
+    def pieces(slot, shares):
+        starts = [0, depth, 2 * depth, 3 * depth, 3 * depth + cut]
+        return [
+            (slot[share], slot[share].shape[0], lambda place: 0, starts[share]) for share in shares
+        ]
+
+    own = [
+        (out_weight, depth, lambda place, share=share: share ^ place[3], share * depth)
+        for share in range(4)
+    ]
     carry = None
-    for distance, slot in enumerate(slots):
+    for distance in range(n_wa):
         block = lax.rem(wa - distance + n_wa, n_wa)
         mine = block // blocks == ta
         inner = lax.rem(block, blocks)
-        place = jnp.stack([mine.astype(jnp.int32), inner, jnp.where(mine, inner, blocks)])
-        total = None
-        for index, part in enumerate(slot):
-            dtype = jnp.bfloat16 if index == len(slot) - 1 else jnp.float32
-            total = project(attended, [p for p, _ in part], [s for _, s in part], total, dtype)
+        place = jnp.stack([mine.astype(jnp.int32), inner, jnp.where(mine, inner, blocks), ha])
+        if distance == 0:
+            total = project(place, attended, own, None, jnp.bfloat16)
+        elif distance < n_wa - 1:
+            total = project(
+                place, attended, pieces(slots[distance - 1], range(5)), None, jnp.bfloat16
+            )
+        else:
+            total = project(
+                place, attended, pieces(slots[distance - 1], range(3)), None, jnp.float32
+            )
+            total = project(
+                place, attended, pieces(slots[distance - 1], range(3, 5)), total, jnp.bfloat16
+            )
         other = swap(total, "ta", 1)
         operands = (place, total, other, hidden, other_hidden, gate, other_gate)
         if distance < n_wa - 1:
@@ -482,7 +538,12 @@
     return finish(*operands, picked[2:3], picked[1:2], carry)
 
 
-def gathered(hidden, attended, out_weight, picked):
+def gathered(hidden, queries, keys_values, windows, out_weight, picked):
+    work = Tokens(queries, keys_values, windows, 1)
+    work.stay()
+    work.visit()
+    work.send_back()
+    attended = work.combine()
     n_ha, n_wa, n_ta = lax.axis_size("ha"), lax.axis_size("wa"), lax.axis_size("ta")
     ha, ta = lax.axis_index("ha"), lax.axis_index("ta")
     tokens, features = attended.shape
@@ -521,10 +582,10 @@
     tokens = math.prod(queries.shape[:3])
     width = hidden_states.shape[3]
     picked = lax.dynamic_index_in_dim(mod_table, step_index[0], 0, keepdims=False)
-    attended = attend_all(queries, keys_values, windows)
-    regular = lax.axis_size("ta") == 2 and lax.axis_size("ha") == 4 and width % LANES == 0
-    residual_out, ffn_input = (paired if regular else gathered)(
-        hidden_states.reshape(tokens, width), attended, out_weight, picked
+    sizes = lax.axis_size("ha"), lax.axis_size("wa"), lax.axis_size("ta")
+    tuned = sizes == (4, 4, 2) and out_weight.shape[0] % (20 * LANES) == 0
+    residual_out, ffn_input = (paired if tuned else gathered)(
+        hidden_states.reshape(tokens, width), queries, keys_values, windows, out_weight, picked
     )
     return residual_out.reshape(hidden_states.shape), ffn_input.reshape(hidden_states.shape)
 

time: 393 us -> 309 us (0.79); the launches traced: 388 us -> 309 us
  starting transfers between devices: 66.9 us -> 31.2 us
  local copies, waits for them, and re-layouts: 35 us -> 14.5 us
  Pallas kernels: 129 us -> 115 us
  waiting for transfers between devices: 155 us -> 146 us
    ppermute x8 -> x6, waiting for transfers between devices: 35.6 us -> 91.8 us  [shift(): return lax.ppermute(block, axis, pairs)]
    ppermute x6 -> x3, waiting for transfers between devices: 77.6 us -> 29.5 us  [turn(): lax.ppermute(block, axis, [(i, (i + step) % count) for i in range(count)])]
    ppermute x30 -> x18, starting transfers between devices: 39.7 us -> 14.3 us  [swap(): return lax.ppermute(block, axis, [(i, i ^ bit) for i in range(count)])]
    ppermute x30 -> x18, waiting for transfers between devices: 42 us -> 25 us  [swap(): return lax.ppermute(block, axis, [(i, i ^ bit) for i in range(count)])]
    pallas_call x7 -> x5, Pallas kernels: 44.3 us -> 29.7 us  [project(): pl.pallas_call(partial(project_kernel, offsets=[piece[3] for piece in pie...]
    unnamed x75 -> x41, local copies, waits for them, and re-layouts: 16.1 us -> 4.34 us
    slice x13 -> x7, local copies, waits for them, and re-layouts: 15.2 us -> 7.5 us  [the longest x6 5.62 us: far_swaps(): return [swap(by_y[:cut], 'ha', 1), swap(by_x[cut:], 'ha', 2)]]
    ppermute x8 -> x6, starting transfers between devices: 20.6 us -> 15.2 us  [shift(): return lax.ppermute(block, axis, pairs)]
  transfers between devices with their start and end apart: 44 -> 27, of which waited for: 10 -> 8; matrix products, arithmetic and copies ran while one was open for 4% -> 3% of each run, Pallas kernels for 31% -> 35%
where the time goes in v3:
time: 309 us
  waiting for transfers between devices  146 us (47%)
  Pallas kernels  115 us (37%)
  starting transfers between devices  31.2 us (10%)
  local copies, waits for them, and re-layouts  14.5 us (5%)
    ppermute x6, waiting for transfers between devices, shift(): return lax.ppermute(block, axis, pairs)  91.8 us
    pallas_call x2, Pallas kernels, attention(): pl.pallas_call(partial(attention_kernel, q_count=q_count, columns_only=co...  52.2 us
    pallas_call x5, Pallas kernels, project(): pl.pallas_call(partial(project_kernel, offsets=[piece[3] for piece in pie...  29.7 us
    ppermute x3, waiting for transfers between devices, turn(): lax.ppermute(block, axis, [(i, (i + step) % count) for i in range(count)])  29.5 us
    ppermute x18, waiting for transfers between devices, swap(): return lax.ppermute(block, axis, [(i, i ^ bit) for i in range(count)])  25 us
    ppermute x6, starting transfers between devices, shift(): return lax.ppermute(block, axis, pairs)  15.2 us
    ppermute x18, starting transfers between devices, swap(): return lax.ppermute(block, axis, [(i, i ^ bit) for i in range(count)])  14.3 us
    pallas_call x3, Pallas kernels, mix(): pl.pallas_call(mix_kernel, grid_spec=pltpu.PrefetchScalarGridSpec(num_sca...  13.4 us
  transfers between devices with their start and end apart: 27, of which 8 were waited for; matrix products, arithmetic and copies ran while one was open for 3% of the time, Pallas kernels for 35%

profile of v3, /device:TPU:17, one launch (start us, length us, event | category | flops | bytes accessed | tf_op | source)
XLA Modules:
  0.0 309.2 jit_solution(17457296261853868326)
XLA Ops:
  5.4 3.2 %collective-permute-start.1 = (bf16[2,2,8,8,2560]{4,3,2,1,0:T(8,128)(2,1)S(1)}, bf16[2,2,8,8,2560]{4,3,2,1,0:T(8,128)(2,1)S(1)}, u32[]{:S(2)}, u32[]{:S(2)}) collective-permute-start(bf16[2,2,8,8,2560]{4,3,2,1,0:T(8,128)(2,1)S(1)} %get-tuple-element.37), channel_id=1, source_target_pairs={{0,8},{8,16},{16,24},{1,9},{9,17},{17,25},{2,10},{10,18},{18,26},{... | collective-permute-start | bytes 3932168 | tf_op jit(solution)/shard_map/ppermute | solution.py:375
  11.9 3.4 %collective-permute-start.7 = (bf16[2,24,8,2560]{3,2,1,0:T(8,128)(2,1)}, bf16[2,24,8,2560]{3,2,1,0:T(8,128)(2,1)}, u32[]{:S(2)}, u32[]{:S(2)}) collective-permute-start(bf16[2,24,8,2560]{3,2,1,0:T(8,128)(2,1)} %param.8), channel_id=1, source_target_pairs={{2,0},{4,2},{6,4},{3,1},{5,3},{7,5},{10,8},{12,10},{14,12},{11,9},... | collective-permute-start | bytes 5898248 | tf_op jit(solution)/shard_map/ppermute | solution.py:375
  15.2 20.4 %collective-permute-done.1 = bf16[2,2,8,8,2560]{4,3,2,1,0:T(8,128)(2,1)S(1)} collective-permute-done((bf16[2,2,8,8,2560]{4,3,2,1,0:T(8,128)(2,1)S(1)}, bf16[2,2,8,8,2560]{4,3,2,1,0:T(8,128)(2,1)S(1)}, u32[]{:S(2)}, u32[]{:S(2)}) %collective-permute-start.1) | collective-permute-done | bytes 1310752 | tf_op jit(solution)/shard_map/ppermute | solution.py:375
  35.7 30.1 %collective-permute-done.2 = bf16[2,2,8,8,2560]{4,3,2,1,0:T(8,128)(2,1)S(1)} collective-permute-done((bf16[2,2,8,8,2560]{4,3,2,1,0:T(8,128)(2,1)S(1)}, bf16[2,2,8,8,2560]{4,3,2,1,0:T(8,128)(2,1)S(1)}, u32[]{:S(2)}, u32[]{:S(2)}) %collective-permute-start.2) | collective-permute-done | bytes 1310752 | tf_op jit(solution)/shard_map/ppermute | solution.py:375
  67.2 22.0 %attend_own.1.own.own_stat = bf16[2,192,2688]{2,1,0:T(8,128)(2,1)} custom-call(s32[20,2]{1,0:T(8,128)S(1)} %copy.11.windows, s32[5]{0:T(128)S(1)} %stack.108.edges, bf16[2,192,2560]{2,1,0:T(8,128)(2,1)} %bitcast.10.refs_0_, bf16[2,2,192,2560]{3,2,1,0:T(8,128)(2,1)} %bitcast.46, bf16[2,2,64,2560]{3,2,1,0:T(8,128)(2,1)S(1)} %bitcast.42, ...), custom_call_target="tpu_custom_call" | custom-call | flops 1 | bytes 1 | tf_op jit(solution)/shard_map/attend_own/pallas_call | solution.py:137
  89.3 12.3 %collective-permute-done.4.refs_1_ = bf16[640,1280]{1,0:T(8,128)(2,1)} collective-permute-done((bf16[640,1280]{1,0:T(8,128)(2,1)}, bf16[640,1280]{1,0:T(8,128)(2,1)}, u32[]{:S(2)}, u32[]{:S(2)}) %collective-permute-start.4) | collective-permute-done | bytes 1638432 | tf_op jit(solution)/shard_map/ppermute | solution.py:385
  105.5 30.1 %attend_neighbours.1 = (bf16[2,192,2688]{2,1,0:T(8,128)(2,1)}, bf16[2,192,2688]{2,1,0:T(8,128)(2,1)}) custom-call(s32[20,2]{1,0:T(8,128)S(1)} %copy.11.windows, s32[5]{0:T(128)S(1)} %stack.108.edges, bf16[2,192,2560]{2,1,0:T(8,128)(2,1)} %bitcast.12.refs_0_, bf16[2,192,2560]{2,1,0:T(8,128)(2,1)} %bitcast.13.refs_1_, bf16[2,2,192,2560]{3,2,1,0:T(8,128)(2,1)} %bitcast.47, ...), custom_call_target="tpu_custom_call" | custom-call | flops 1 | bytes 1 | tf_op jit(solution)/shard_map/attend_neighbours/pallas_call | solution.py:137
  139.4 2.8 collective-permute-start.15
  142.2 2.6 collective-permute-start.16
  144.9 29.5 %collective-permute-done.10.refs_0_ = bf16[640,1280]{1,0:T(8,128)(2,1)S(1)} collective-permute-done((bf16[640,1280]{1,0:T(8,128)(2,1)}, bf16[640,1280]{1,0:T(8,128)(2,1)S(1)}, u32[]{:S(2)}, u32[]{:S(2)}) %collective-permute-start.10) | collective-permute-done | bytes 1638432 | tf_op jit(solution)/shard_map/ppermute | solution.py:380
  177.3 41.3 %collective-permute-done.15.left.left_stat = bf16[2,192,2688]{2,1,0:T(8,128)(2,1)S(1)} collective-permute-done((bf16[2,192,2688]{2,1,0:T(8,128)(2,1)}, bf16[2,192,2688]{2,1,0:T(8,128)(2,1)S(1)}, u32[]{:S(2)}, u32[]{:S(2)}) %collective-permute-start.15) | collective-permute-done | bytes 2064416 | tf_op jit(solution)/shard_map/ppermute | solution.py:375
  218.6 2.3 collective-permute-start.22
  220.9 12.3 %collective-permute-done.17.refs_3_ = bf16[256,1280]{1,0:T(8,128)(2,1)S(1)} collective-permute-done((bf16[256,1280]{1,0:T(8,128)(2,1)S(1)}, bf16[256,1280]{1,0:T(8,128)(2,1)S(1)}, u32[]{:S(2)}, u32[]{:S(2)}) %collective-permute-start.17) | collective-permute-done | bytes 655392 | tf_op jit(solution)/shard_map/ppermute | solution.py:385
  234.1 13.4 %combine.1 = bf16[2,192,2560]{2,1,0:T(8,128)(2,1)S(1)} custom-call(s32[20,2]{1,0:T(8,128)S(1)} %copy.11.windows, s32[5]{0:T(128)S(1)} %stack.108.edges, bf16[2,192,2688]{2,1,0:T(8,128)(2,1)S(1)} %copy-done.2, bf16[2,192,2688]{2,1,0:T(8,128)(2,1)S(1)} %collective-permute-done.15.left.left_stat, bf16[2,192,2688]{2,1,0:T(8,128)(2,1)} %copy-done.17, ...), custom_call_target="tpu_custom_call" | custom-call | flops 1 | bytes 1 | tf_op jit(solution)/shard_map/combine/pallas_call | solution.py:207
  254.7 3.0 collective-permute-start.23
  258.0 6.4 %project.9.own_part = bf16[384,1280]{1,0:T(8,128)(2,1)S(1)} custom-call(s32[4]{0:T(128)S(1)} %add_add_fusion.3.place, bf16[384,2560]{1,0:T(8,128)(2,1)S(1)} %bitcast.37, bf16[2560,1280]{1,0:T(8,128)(2,1)} %refs_3_.1, bf16[2560,1280]{1,0:T(8,128)(2,1)} %refs_3_.1, bf16[2560,1280]{1,0:T(8,128)(2,1)} %refs_3_.1, bf16[2560,1280]{1,0:T(8,128)(2,1)} %refs_3_.1), custom_call_target="tpu_custom_call" | custom-call | flops 1 | bytes 1 | tf_op jit(solution)/shard_map/project/pallas_call | solution.py:246
  264.7 6.8 %project.8.own_part = bf16[384,1280]{1,0:T(8,128)(2,1)S(1)} custom-call(s32[4]{0:T(128)S(1)} %add_add_fusion.2.place, bf16[384,2560]{1,0:T(8,128)(2,1)} %bitcast.38, bf16[640,1280]{1,0:T(8,128)(2,1)} %collective-permute-done.refs_0_, bf16[640,1280]{1,0:T(8,128)(2,1)} %collective-permute-done.4.refs_1_, bf16[640,1280]{1,0:T(8,128)(2,1)} %collective-permute-done.5.refs_2_, ...), custom_call_target="tpu_custom_call" | custom-call | flops 1 | bytes 1 | tf_op jit(solution)/shard_map/project/pallas_call | solution.py:246
  272.0 6.9 %project.7.own_part = bf16[384,1280]{1,0:T(8,128)(2,1)S(1)} custom-call(s32[4]{0:T(128)S(1)} %add_add_fusion.1.place, bf16[384,2560]{1,0:T(8,128)(2,1)} %bitcast.39, bf16[640,1280]{1,0:T(8,128)(2,1)} %collective-permute-done.3.refs_0_, bf16[640,1280]{1,0:T(8,128)(2,1)S(1)} %copy-done.4, bf16[640,1280]{1,0:T(8,128)(2,1)} %copy-done.18, ...), custom_call_target="tpu_custom_call" | custom-call | flops 1 | bytes 1 | tf_op jit(solution)/shard_map/project/pallas_call | solution.py:246
  279.4 6.2 %project.5.refs_2_ = f32[384,1280]{1,0:T(8,128)} custom-call(s32[4]{0:T(128)S(1)} %add_add_fusion.place, bf16[384,2560]{1,0:T(8,128)(2,1)} %bitcast.40, bf16[640,1280]{1,0:T(8,128)(2,1)S(1)} %copy-done.10, bf16[640,1280]{1,0:T(8,128)(2,1)S(1)} %copy-done.6, bf16[640,1280]{1,0:T(8,128)(2,1)S(1)} %copy-done.8), custom_call_target="tpu_custom_call" | custom-call | flops 1 | bytes 1 | tf_op jit(solution)/shard_map/project/pallas_call | solution.py:246
  285.6 3.3 %project.6.own_part = bf16[384,1280]{1,0:T(8,128)(2,1)S(1)} custom-call(s32[4]{0:T(128)S(1)} %add_add_fusion.place, bf16[384,2560]{1,0:T(8,128)(2,1)S(1)} %bitcast.41, bf16[256,1280]{1,0:T(8,128)(2,1)} %collective-permute-done.19.refs_0_, bf16[384,1280]{1,0:T(8,128)(2,1)} %collective-permute-done.20.refs_1_, f32[384,1280]{1,0:T(8,128)} %project.5.refs_2_), custom_call_target="tpu_custom_call" | custom-call | flops 1 | bytes 1 | tf_op jit(solution)/shard_map/project/pallas_call | solution.py:246
  289.2 4.5 %mix.3 = (f32[384,3840]{1,0:T(8,128)}, f32[384,128]{1,0:T(8,128)S(1)}) custom-call(s32[4]{0:T(128)S(1)} %add_add_fusion.3.place, bf16[384,1280]{1,0:T(8,128)(2,1)S(1)} %project.9.own_part, bf16[384,1280]{1,0:T(8,128)(2,1)S(1)} %collective-permute-done.26.other_part, bf16[384,2560]{1,0:T(8,128)(2,1)} %bitcast.15.own_hidden, ...), custom_call_target="tpu_custom_call" | custom-call | flops 1 | bytes 1 | tf_op jit(solution)/shard_map/mix/pallas_call | solution.py:295
  293.7 4.5 %mix.4 = (f32[384,3840]{1,0:T(8,128)}, f32[384,128]{1,0:T(8,128)S(1)}) custom-call(s32[4]{0:T(128)S(1)} %add_add_fusion.2.place, bf16[384,1280]{1,0:T(8,128)(2,1)S(1)} %project.8.own_part, bf16[384,1280]{1,0:T(8,128)(2,1)S(1)} %collective-permute-done.25.other_part, bf16[384,2560]{1,0:T(8,128)(2,1)} %bitcast.15.own_hidden, ...), custom_call_target="tpu_custom_call", output_to_operand_aliasing={{0}: (8, {})} | custom-call | flops 1 | bytes 1 | tf_op jit(solution)/shard_map/mix/pallas_call | solution.py:295
  298.2 4.5 %mix.5 = (f32[384,3840]{1,0:T(8,128)}, f32[384,128]{1,0:T(8,128)S(1)}) custom-call(s32[4]{0:T(128)S(1)} %add_add_fusion.1.place, bf16[384,1280]{1,0:T(8,128)(2,1)S(1)} %project.7.own_part, bf16[384,1280]{1,0:T(8,128)(2,1)S(1)} %collective-permute-done.24.other_part, bf16[384,2560]{1,0:T(8,128)(2,1)} %bitcast.15.own_hidden, ...), custom_call_target="tpu_custom_call", output_to_operand_aliasing={{0}: (8, {})} | custom-call | flops 1 | bytes 1 | tf_op jit(solution)/shard_map/mix/pallas_call | solution.py:295
  302.6 6.6 %finish.1 = (bf16[384,2560]{1,0:T(8,128)(2,1)}, bf16[384,2560]{1,0:T(8,128)(2,1)}) custom-call(s32[4]{0:T(128)S(1)} %add_add_fusion.place, bf16[384,1280]{1,0:T(8,128)(2,1)S(1)} %project.6.own_part, bf16[384,1280]{1,0:T(8,128)(2,1)S(1)} %collective-permute-done.21.other_part, bf16[384,2560]{1,0:T(8,128)(2,1)} %bitcast.15.own_hidden, ...), custom_call_target="tpu_custom_call" | custom-call | flops 1 | bytes 1 | tf_op jit(solution)/shard_map/finish/pallas_call | solution.py:354
  (97 shorter events, 29.0 us)
Async XLA Ops:
  2.2 63.6 %collective-permute-start = (bf16[640,1280]{1,0:T(8,128)(2,1)S(1)}, bf16[640,1280]{1,0:T(8,128)(2,1)}, u32[]{:S(2)}, u32[]{:S(2)}) collective-permute-start(bf16[640,1280]{1,0:T(8,128)(2,1)S(1)} %constant_dynamic-slice_fusion), channel_id=1, source_target_pairs={{0,2},{2,4},{4,6},{6,0},{1,3},{3,5},{5,7},{7,1},{8,10},{10,12},{12... | collective-permute-start | bytes 4915208 | tf_op jit(solution)/shard_map/ppermute | solution.py:380
  5.4 30.2 %collective-permute-start.1 = (bf16[2,2,8,8,2560]{4,3,2,1,0:T(8,128)(2,1)S(1)}, bf16[2,2,8,8,2560]{4,3,2,1,0:T(8,128)(2,1)S(1)}, u32[]{:S(2)}, u32[]{:S(2)}) collective-permute-start(bf16[2,2,8,8,2560]{4,3,2,1,0:T(8,128)(2,1)S(1)} %get-tuple-element.37), channel_id=1, source_target_pairs={{0,8},{8,16},{16,24},{1,9},{9,17},{17,25},{2,10},{10,18},{18,26},{... | collective-permute-start | bytes 3932168 | tf_op jit(solution)/shard_map/ppermute | solution.py:375
  8.6 57.2 %collective-permute-start.2 = (bf16[2,2,8,8,2560]{4,3,2,1,0:T(8,128)(2,1)S(1)}, bf16[2,2,8,8,2560]{4,3,2,1,0:T(8,128)(2,1)S(1)}, u32[]{:S(2)}, u32[]{:S(2)}) collective-permute-start(bf16[2,2,8,8,2560]{4,3,2,1,0:T(8,128)(2,1)S(1)} %get-tuple-element.38), channel_id=1, source_target_pairs={{8,0},{16,8},{24,16},{9,1},{17,9},{25,17},{10,2},{18,10},{26,18},{... | collective-permute-start | bytes 3932168 | tf_op jit(solution)/shard_map/ppermute | solution.py:375
  9.9 79.3 %collective-permute-start.6 = (bf16[2,24,8,2560]{3,2,1,0:T(8,128)(2,1)}, bf16[2,24,8,2560]{3,2,1,0:T(8,128)(2,1)}, u32[]{:S(2)}, u32[]{:S(2)}) collective-permute-start(bf16[2,24,8,2560]{3,2,1,0:T(8,128)(2,1)} %param.8), channel_id=1, source_target_pairs={{0,2},{2,4},{4,6},{1,3},{3,5},{5,7},{8,10},{10,12},{12,14},{9,11},... | collective-permute-start | bytes 5898248 | tf_op jit(solution)/shard_map/ppermute | solution.py:375
  11.9 77.4 %collective-permute-start.7 = (bf16[2,24,8,2560]{3,2,1,0:T(8,128)(2,1)}, bf16[2,24,8,2560]{3,2,1,0:T(8,128)(2,1)}, u32[]{:S(2)}, u32[]{:S(2)}) collective-permute-start(bf16[2,24,8,2560]{3,2,1,0:T(8,128)(2,1)} %param.8), channel_id=1, source_target_pairs={{2,0},{4,2},{6,4},{3,1},{5,3},{7,5},{10,8},{12,10},{14,12},{11,9},... | collective-permute-start | bytes 5898248 | tf_op jit(solution)/shard_map/ppermute | solution.py:375
  65.8 35.7 %collective-permute-start.4 = (bf16[640,1280]{1,0:T(8,128)(2,1)}, bf16[640,1280]{1,0:T(8,128)(2,1)}, u32[]{:S(2)}, u32[]{:S(2)}) collective-permute-start(bf16[640,1280]{1,0:T(8,128)(2,1)} %collective-permute-done.refs_0_), channel_id=1, source_target_pairs={{0,8},{8,0},{16,24},{24,16},{1,9},{9,1},{17,25},{25,17},{2,10},{10... | collective-permute-start | bytes 4915208 | tf_op jit(solution)/shard_map/ppermute | solution.py:385
  66.9 34.8 %collective-permute-start.5 = (bf16[640,1280]{1,0:T(8,128)(2,1)}, bf16[640,1280]{1,0:T(8,128)(2,1)}, u32[]{:S(2)}, u32[]{:S(2)}) collective-permute-start(bf16[640,1280]{1,0:T(8,128)(2,1)} %collective-permute-done.refs_0_), channel_id=1, source_target_pairs={{0,16},{8,24},{16,0},{24,8},{1,17},{9,25},{17,1},{25,9},{2,18},{10... | collective-permute-start | bytes 4915208 | tf_op jit(solution)/shard_map/ppermute | solution.py:385
  66.9 68.7 %collective-permute-start.3 = (bf16[640,1280]{1,0:T(8,128)(2,1)}, bf16[640,1280]{1,0:T(8,128)(2,1)}, u32[]{:S(2)}, u32[]{:S(2)}) collective-permute-start(bf16[640,1280]{1,0:T(8,128)(2,1)} %collective-permute-done.refs_0_), channel_id=1, source_target_pairs={{0,2},{2,4},{4,6},{6,0},{1,3},{3,5},{5,7},{7,1},{8,10},{10,12},{12... | collective-permute-start | bytes 4915208 | tf_op jit(solution)/shard_map/ppermute | solution.py:380
  103.0 33.5 %collective-permute-start.9 = (bf16[384,1280]{1,0:T(8,128)(2,1)S(1)}, bf16[384,1280]{1,0:T(8,128)(2,1)S(1)}, u32[]{:S(2)}, u32[]{:S(2)}) collective-permute-start(bf16[384,1280]{1,0:T(8,128)(2,1)S(1)} %slice.45), channel_id=1, source_target_pairs={{0,16},{8,24},{16,0},{24,8},{1,17},{9,25},{17,1},{25,9},{2,18},{10... | collective-permute-start | bytes 2949128 | tf_op jit(solution)/shard_map/ppermute | solution.py:385
  104.5 31.1 %collective-permute-start.8 = (bf16[256,1280]{1,0:T(8,128)(2,1)S(1)}, bf16[256,1280]{1,0:T(8,128)(2,1)S(1)}, u32[]{:S(2)}, u32[]{:S(2)}) collective-permute-start(bf16[256,1280]{1,0:T(8,128)(2,1)S(1)} %slice.44), channel_id=1, source_target_pairs={{0,8},{8,0},{16,24},{24,16},{1,9},{9,1},{17,25},{25,17},{2,10},{10... | collective-permute-start | bytes 1966088 | tf_op jit(solution)/shard_map/ppermute | solution.py:385
  137.4 36.9 %collective-permute-start.10 = (bf16[640,1280]{1,0:T(8,128)(2,1)}, bf16[640,1280]{1,0:T(8,128)(2,1)S(1)}, u32[]{:S(2)}, u32[]{:S(2)}) collective-permute-start(bf16[640,1280]{1,0:T(8,128)(2,1)} %collective-permute-done.3.refs_0_), channel_id=1, source_target_pairs={{0,2},{2,4},{4,6},{6,0},{1,3},{3,5},{5,7},{7,1},{8,10},{10,12},{12... | collective-permute-start | bytes 4915208 | tf_op jit(solution)/shard_map/ppermute | solution.py:380
  137.7 36.8 %collective-permute-start.11 = (bf16[640,1280]{1,0:T(8,128)(2,1)}, bf16[640,1280]{1,0:T(8,128)(2,1)S(1)}, u32[]{:S(2)}, u32[]{:S(2)}) collective-permute-start(bf16[640,1280]{1,0:T(8,128)(2,1)} %collective-permute-done.3.refs_0_), channel_id=1, source_target_pairs={{0,8},{8,0},{16,24},{24,16},{1,9},{9,1},{17,25},{25,17},{2,10},{10... | collective-permute-start | bytes 4915208 | tf_op jit(solution)/shard_map/ppermute | solution.py:385
  138.2 36.2 %collective-permute-start.12 = (bf16[640,1280]{1,0:T(8,128)(2,1)}, bf16[640,1280]{1,0:T(8,128)(2,1)S(1)}, u32[]{:S(2)}, u32[]{:S(2)}) collective-permute-start(bf16[640,1280]{1,0:T(8,128)(2,1)} %collective-permute-done.3.refs_0_), channel_id=1, source_target_pairs={{0,16},{8,24},{16,0},{24,8},{1,17},{9,25},{17,1},{25,9},{2,18},{10... | collective-permute-start | bytes 4915208 | tf_op jit(solution)/shard_map/ppermute | solution.py:385
  139.4 79.2 %collective-permute-start.15 = (bf16[2,192,2688]{2,1,0:T(8,128)(2,1)}, bf16[2,192,2688]{2,1,0:T(8,128)(2,1)S(1)}, u32[]{:S(2)}, u32[]{:S(2)}) collective-permute-start(bf16[2,192,2688]{2,1,0:T(8,128)(2,1)} %get-tuple-element.51), channel_id=1, source_target_pairs={{0,2},{2,4},{4,6},{1,3},{3,5},{5,7},{8,10},{10,12},{12,14},{9,11},... | collective-permute-start | bytes 6193160 | tf_op jit(solution)/shard_map/ppermute | solution.py:375
  142.2 76.3 %collective-permute-start.16 = (bf16[2,192,2688]{2,1,0:T(8,128)(2,1)}, bf16[2,192,2688]{2,1,0:T(8,128)(2,1)S(1)}, u32[]{:S(2)}, u32[]{:S(2)}) collective-permute-start(bf16[2,192,2688]{2,1,0:T(8,128)(2,1)} %get-tuple-element.52), channel_id=1, source_target_pairs={{2,0},{4,2},{6,4},{3,1},{5,3},{7,5},{10,8},{12,10},{14,12},{11,9},... | collective-permute-start | bytes 6193160 | tf_op jit(solution)/shard_map/ppermute | solution.py:375
  174.5 73.1 %collective-permute-start.13 = (bf16[640,1280]{1,0:T(8,128)(2,1)S(1)}, bf16[640,1280]{1,0:T(8,128)(2,1)S(1)}, u32[]{:S(2)}, u32[]{:S(2)}) collective-permute-start(bf16[640,1280]{1,0:T(8,128)(2,1)S(1)} %collective-permute-done.10.refs_0_), channel_id=1, source_target_pairs={{0,8},{8,0},{16,24},{24,16},{1,9},{9,1},{17,25},{25,17},{2,10},{10... | collective-permute-start | bytes 4915208 | tf_op jit(solution)/shard_map/ppermute | solution.py:385
  175.6 72.0 %collective-permute-start.14 = (bf16[640,1280]{1,0:T(8,128)(2,1)S(1)}, bf16[640,1280]{1,0:T(8,128)(2,1)S(1)}, u32[]{:S(2)}, u32[]{:S(2)}) collective-permute-start(bf16[640,1280]{1,0:T(8,128)(2,1)S(1)} %collective-permute-done.10.refs_0_), channel_id=1, source_target_pairs={{0,16},{8,24},{16,0},{24,8},{1,17},{9,25},{17,1},{25,9},{2,18},{10... | collective-permute-start | bytes 4915208 | tf_op jit(solution)/shard_map/ppermute | solution.py:385
  176.7 57.4 %collective-permute-start.18 = (bf16[384,1280]{1,0:T(8,128)(2,1)S(1)}, bf16[384,1280]{1,0:T(8,128)(2,1)S(1)}, u32[]{:S(2)}, u32[]{:S(2)}) collective-permute-start(bf16[384,1280]{1,0:T(8,128)(2,1)S(1)} %slice.47), channel_id=1, source_target_pairs={{0,16},{8,24},{16,0},{24,8},{1,17},{9,25},{17,1},{25,9},{2,18},{10... | collective-permute-start | bytes 2949128 | tf_op jit(solution)/shard_map/ppermute | solution.py:385
  218.6 70.6 %collective-permute-start.22 = (bf16[384,2560]{1,0:T(8,128)(2,1)}, bf16[384,2560]{1,0:T(8,128)(2,1)}, u32[]{:S(2)}, u32[]{:S(2)}) collective-permute-start(bf16[384,2560]{1,0:T(8,128)(2,1)} %bitcast.15.own_hidden), channel_id=1, source_target_pairs={{0,1},{1,0},{2,3},{3,2},{4,5},{5,4},{6,7},{7,6},{8,9},{9,8},{10,11... | collective-permute-start | bytes 5898248 | tf_op jit(solution)/shard_map/ppermute | solution.py:385
  250.3 28.6 %collective-permute-start.20 = (bf16[384,1280]{1,0:T(8,128)(2,1)}, bf16[384,1280]{1,0:T(8,128)(2,1)}, u32[]{:S(2)}, u32[]{:S(2)}) collective-permute-start(bf16[384,1280]{1,0:T(8,128)(2,1)} %slice.49), channel_id=1, source_target_pairs={{0,16},{8,24},{16,0},{24,8},{1,17},{9,25},{17,1},{25,9},{2,18},{10... | collective-permute-start | bytes 2949128 | tf_op jit(solution)/shard_map/ppermute | solution.py:385
  254.7 34.3 %collective-permute-start.23 = (f32[1,2560]{1,0:T(1,128)S(1)}, f32[1,2560]{1,0:T(1,128)S(1)}, u32[]{:S(2)}, u32[]{:S(2)}) collective-permute-start(f32[1,2560]{1,0:T(1,128)S(1)} %get-tuple-element.76.own_gate), channel_id=1, source_target_pairs={{0,1},{1,0},{2,3},{3,2},{4,5},{5,4},{6,7},{7,6},{8,9},{9,8},{10,11... | collective-permute-start | bytes 30728 | tf_op jit(solution)/shard_map/ppermute | solution.py:385
  264.5 24.7 %collective-permute-start.26 = (bf16[384,1280]{1,0:T(8,128)(2,1)S(1)}, bf16[384,1280]{1,0:T(8,128)(2,1)S(1)}, u32[]{:S(2)}, u32[]{:S(2)}) collective-permute-start(bf16[384,1280]{1,0:T(8,128)(2,1)S(1)} %project.9.own_part), channel_id=1, source_target_pairs={{0,1},{1,0},{2,3},{3,2},{4,5},{5,4},{6,7},{7,6},{8,9},{9,8},{10,11... | collective-permute-start | bytes 2949128 | tf_op jit(solution)/shard_map/ppermute | solution.py:385
  271.5 22.1 %collective-permute-start.25 = (bf16[384,1280]{1,0:T(8,128)(2,1)S(1)}, bf16[384,1280]{1,0:T(8,128)(2,1)S(1)}, u32[]{:S(2)}, u32[]{:S(2)}) collective-permute-start(bf16[384,1280]{1,0:T(8,128)(2,1)S(1)} %project.8.own_part), channel_id=1, source_target_pairs={{0,1},{1,0},{2,3},{3,2},{4,5},{5,4},{6,7},{7,6},{8,9},{9,8},{10,11... | collective-permute-start | bytes 2949128 | tf_op jit(solution)/shard_map/ppermute | solution.py:385
  278.9 19.2 %collective-permute-start.24 = (bf16[384,1280]{1,0:T(8,128)(2,1)S(1)}, bf16[384,1280]{1,0:T(8,128)(2,1)S(1)}, u32[]{:S(2)}, u32[]{:S(2)}) collective-permute-start(bf16[384,1280]{1,0:T(8,128)(2,1)S(1)} %project.7.own_part), channel_id=1, source_target_pairs={{0,1},{1,0},{2,3},{3,2},{4,5},{5,4},{6,7},{7,6},{8,9},{9,8},{10,11... | collective-permute-start | bytes 2949128 | tf_op jit(solution)/shard_map/ppermute | solution.py:385
  (23 other events, 455.2 us)
